TPU v7x, 32 devices: a whole 2x2x4 slice. The times are simulated.
32 devices in a mesh: space: 8 (over y, x, core), sample: 4 (over z).
Axes of the slice: x: 2, y: 2, z: 4, core: 2. Of those that a mesh axis runs over, the one named last changes fastest.
Arguments:
- ensemble: bfloat16 [48, 4, 1024, 1024], P(None, 'sample', 'space'), may hold values from -6 to 6
- map_one: bfloat16 [1024, 256], P('space'), may hold values from -0.1875 to 0.1875
- map_two: bfloat16 [1024, 256], replicated, may hold values from -0.1875 to 0.1875
- map_three: bfloat16 [48, 256], replicated, may hold values from -0.875 to 0.875
- map_four: bfloat16 [4, 256], P('sample'), may hold values from -3 to 3
- core_one: bfloat16 [1024, 128], replicated, may hold values from -0.1875 to 0.1875
- core_two: bfloat16 [1024, 128], replicated, may hold values from -0.1875 to 0.1875
- core_three: bfloat16 [48, 128], replicated, may hold values from -0.875 to 0.875
- core_four: bfloat16 [4, 128], replicated, may hold values from -3 to 3
Outputs:
- sketch_one: float32 [1024, 256], P('space', 'sample')
- sketch_two: float32 [1024, 256], P(('space', 'sample'))
- sketch_three: float32 [48, 256], replicated
- sketch_four: float32 [4, 256], P('sample')
- core_sketch: float32 [128, 16384, 128], P(None, ('space', 'sample'))
All inputs are finite; a program needn't handle non-finite values.
Results may differ from a plain program's by a relative error of at most 0.0029.
Values sent between devices are 32-bit elements; how exact they have to be, the bound alone decides.
No kernel may reach another device: no remote copies, remote signals or barrier semaphores. Data moves between devices by JAX's collectives and lax.ppermute only.
A program may use at most 128 MiB of HBM per device.

v0:
```python
import functools

import jax
import jax.numpy as jnp
from jax import lax
from jax.experimental import pallas as pl
from jax.experimental.pallas import tpu as pltpu
from jax.sharding import PartitionSpec as P

BF16 = jnp.bfloat16
F32 = jnp.float32
NT = (((1,), (1,)), ((), ()))
MIB = 1 << 20
CHUNKS = 1
SPAN, SLOTS = 4, 4
LIGHT = pl.CostEstimate(flops=1, bytes_accessed=1, transcendentals=0)


def split(value):
    high = value.astype(BF16)
    return high, (value - high.astype(F32)).astype(BF16)


def core_kernel(
    space, sample, block, chunks, x_hbm, two_hbm, one_hbm, *refs
):
    outs, (x_ref, two_ref, one_ref, left_ref, right_ref, sems) = refs[: 2 * chunks], refs[2 * chunks :]
    times, points, _ = x_ref.shape
    rank = two_ref.shape[1]
    half = rank // 2
    count = times // block
    me, my = lax.axis_index("space"), lax.axis_index("sample")
    copies = [
        pltpu.make_async_copy(two_hbm, two_ref, sems.at[count]),
        pltpu.make_async_copy(
            one_hbm.at[pl.ds(pl.multiple_of(me * points, points), points)], one_ref, sems.at[count + 1]
        ),
    ]
    loads = [
        pltpu.make_async_copy(
            x_hbm.at[pl.ds(n * block, block), 0], x_ref.at[pl.ds(n * block, block)], sems.at[n]
        )
        for n in range(count)
    ]
    for copy in copies + loads:
        copy.start()
    own = rank // (space * sample)
    piece = own // chunks
    slot = lax.broadcasted_iota(jnp.int32, (rank, rank), 0)
    column = lax.broadcasted_iota(jnp.int32, (rank, rank), 1)
    odd = slot // half
    rest = slot % half
    part = rest // (half // chunks)
    rest = rest % (half // chunks)
    inner = rest % piece
    far = (rest // piece) % sample
    chip = rest // (piece * sample)
    place = ((chip * 2 + odd) ^ me) * sample + (far ^ my)
    pick = jnp.where(column == place * own + part * piece + inner, 1.0, 0.0).astype(BF16)
    groups = sample
    wide = rank // groups
    row = lax.broadcasted_iota(jnp.int32, (rank, rank), 0)
    group, within = column // wide, column % wide
    source = (within // 2) * (2 * groups) + 2 * group + within % 2
    order = jnp.where(row == source, 1.0, 0.0).astype(BF16)
    for copy in copies:
        copy.wait()
    left_ref[...] = lax.dot_general(
        pick, two_ref[...], NT, preferred_element_type=F32
    ).astype(BF16)
    ordered = jnp.dot(one_ref[...], order, preferred_element_type=F32).astype(BF16)
    right_ref[...] = jnp.concatenate([ordered, ordered], axis=0)

    for n in range(count):
        loads[n].wait()
        x = x_ref[n * block : (n + 1) * block].reshape(block * points, x_ref.shape[2])
        first = lax.dot_general(left_ref[...], x, NT, preferred_element_type=F32)
        rows = []
        for t in range(block):
            high, low = split(first[:, t * points : (t + 1) * points])
            rows.append(jnp.concatenate([high, low], axis=1))
        out = jnp.dot(
            jnp.concatenate(rows, axis=0), right_ref[...], preferred_element_type=F32
        )
        size = half // chunks
        for t in range(block):
            for k in range(2 * chunks):
                at = t * rank + k * size
                outs[k][pl.ds(n * block + t, size, stride=times), :] = out[at : at + size]


def core_partial(ensemble, core_one, core_two, space, sample, block, chunks):
    times, _, points, width = ensemble.shape
    rank = core_two.shape[1]
    shape = jax.ShapeDtypeStruct((rank // 2 // chunks * times, rank), F32)
    hbm = pl.BlockSpec(memory_space=pltpu.HBM)
    return pl.pallas_call(
        functools.partial(core_kernel, space, sample, block, chunks),
        in_specs=[hbm] * 3,
        out_specs=[pl.BlockSpec(memory_space=pltpu.VMEM)] * (2 * chunks),
        out_shape=[shape] * (2 * chunks),
        scratch_shapes=[
            pltpu.VMEM((times, points, width), BF16),
            pltpu.VMEM(core_two.shape, BF16),
            pltpu.VMEM((points, rank), BF16),
            pltpu.VMEM((rank, width), BF16),
            pltpu.VMEM((2 * points, rank), BF16),
            pltpu.SemaphoreType.DMA((times // block + 2,)),
        ],
        compiler_params=pltpu.CompilerParams(vmem_limit_bytes=28 * MIB),
        cost_estimate=LIGHT,
        name="core_partial",
    )(
        pltpu.with_memory_space_constraint(ensemble, pltpu.HBM),
        pltpu.with_memory_space_constraint(core_two, pltpu.HBM),
        pltpu.with_memory_space_constraint(core_one, pltpu.HBM),
    )


def sketch_kernel(
    space, sample, block, x_hbm, one_ref, two_ref, three_ref, four_ref, after_ref,
    keep_ref, send_ref, first_ref,
    x_ref, acc_one, acc_two, acc_u, pairs, rolled, one_t, turned, sems,
):
    del after_ref
    times, points, cols = x_ref.shape
    width = two_ref.shape[1]
    count = times // block
    loads = [
        pltpu.make_async_copy(
            x_hbm.at[pl.ds(n * block, block), 0], x_ref.at[pl.ds(n * block, block)], sems.at[n]
        )
        for n in range(count)
    ]
    for load in loads:
        load.start()
    acc_one[...] = jnp.zeros_like(acc_one)
    acc_two[...] = jnp.zeros_like(acc_two)
    four = four_ref[...].astype(F32)
    pair = three_ref[...].astype(F32) * four
    pairs[...] = pair.reshape(pairs.shape)
    padded = jnp.concatenate([pair, jnp.zeros((128 - times, width), F32)], axis=0)
    flipped = padded.T
    for n in range(count):
        rolled[n] = pltpu.roll(flipped, (128 - n * block) % 128, 1)
    one = one_ref[...].astype(F32)
    if points < 128:
        one = jnp.concatenate([one, jnp.zeros((128 - points, width), F32)], axis=0)
    one_t[...] = one.T[:, :points]

    for step in range(count):
        loads[step].wait()
        x = x_ref[step * block : (step + 1) * block].reshape(block * points, cols)
        proj = jnp.dot(x, two_ref[...], preferred_element_type=F32)
        one = one_ref[...].astype(F32)
        weights = rolled[step]
        total = acc_one[...]
        sums, krao = [], []
        for t in range(block):
            part = proj[t * points : (t + 1) * points]
            total = total + part * pairs[step, t : t + 1, :]
            sums.append(jnp.sum(part * one, axis=0, keepdims=True))
            krao.append((weights[:, t : t + 1] * one_t[...]).astype(BF16))
        acc_one[...] = total
        acc_u[step] = jnp.concatenate(sums, axis=0)
        acc_two[...] += jnp.dot(
            jnp.concatenate(krao, axis=1), x, preferred_element_type=F32
        )

    me, my = lax.axis_index("space"), lax.axis_index("sample")
    turned[...] = acc_two[...].T
    own = cols // (space * sample)
    for slot in range(space):
        ref = send_ref if slot % 2 else keep_ref
        for far in range(sample):
            place = (slot ^ me) * sample + (far ^ my)
            at = (slot // 2 * sample + far) * own
            ref[at : at + own, :] = turned[pl.ds(pl.multiple_of(place * own, own), own), :]
    u = acc_u[...].reshape(times, width)
    three = three_ref[...].astype(F32)
    tail = space // 2 * sample * own
    third = u * four_ref[...].astype(F32)
    fourth = jnp.sum(u * three, axis=0, keepdims=True)
    fourth = jnp.concatenate([fourth, jnp.zeros((7, width), F32)], axis=0)
    for ref in (keep_ref, send_ref):
        ref[tail : tail + times, :] = third
        ref[tail + times :, :] = fourth
    narrow, folds = width // sample, width // points
    lines = narrow // folds
    square = acc_one[...]
    if points < 128:
        square = jnp.concatenate([square, jnp.zeros((128 - points, width), F32)], axis=0)
    turned[:width, :128] = square.T
    for far in range(sample):
        at = (far ^ my) * narrow
        pieces = [
            turned[pl.ds(pl.multiple_of(at + n * lines, 8), lines), :points] for n in range(folds)
        ]
        first_ref[far] = jnp.concatenate(pieces, axis=1)


def sketch_partial(
    ensemble, map_one, map_two, map_three, map_four, after, space, sample, block
):
    times, _, points, cols = ensemble.shape
    width = map_two.shape[1]
    own = cols // (space * sample)
    shape = jax.ShapeDtypeStruct((space // 2 * sample * own + times + 8, width), F32)
    first = jax.ShapeDtypeStruct((sample, points // sample, width), F32)
    anywhere = pl.BlockSpec(memory_space=pl.ANY)
    return pl.pallas_call(
        functools.partial(sketch_kernel, space, sample, block),
        in_specs=[pl.BlockSpec(memory_space=pltpu.HBM)]
        + [pl.BlockSpec(memory_space=pltpu.VMEM)] * 4
        + [anywhere],
        out_specs=[pl.BlockSpec(memory_space=pltpu.VMEM)] * 3,
        out_shape=[shape, shape, first],
        scratch_shapes=[
            pltpu.VMEM((times, points, cols), BF16),
            pltpu.VMEM((points, width), F32),
            pltpu.VMEM((width, cols), F32),
            pltpu.VMEM((times // block, block, width), F32),
            pltpu.VMEM((times // block, block, width), F32),
            pltpu.VMEM((times // block, width, 128), F32),
            pltpu.VMEM((width, points), F32),
            pltpu.VMEM((cols, width), F32),
            pltpu.SemaphoreType.DMA((times // block,)),
        ],
        compiler_params=pltpu.CompilerParams(vmem_limit_bytes=32 * MIB),
        cost_estimate=LIGHT,
        name="sketch_partial",
    )(
        pltpu.with_memory_space_constraint(ensemble, pltpu.HBM),
        map_one, map_two, map_three, map_four, after,
    )


def final_kernel(sample, place, *refs):
    start, first, count, _ = place
    *ins, out_hbm, token_ref, left_ref, base_ref, ring, sems = refs
    parts, (three_ref, four_ref) = ins[:sample], ins[sample : sample + 2]
    times, rank = three_ref.shape
    wide = rank // sample
    slots, each = ring.shape[0], ring.shape[1]
    span = each // (2 * sample)
    my = lax.axis_index("sample")

    token_ref[...] = jnp.zeros_like(token_ref)
    three = three_ref[...].astype(F32)
    three = jnp.concatenate([three, jnp.zeros((rank - times, rank), F32)], axis=0).T
    three = three[:, :times].astype(BF16)
    three = jnp.concatenate([three, three], axis=1)
    four = four_ref[...].astype(F32)
    which = lax.broadcasted_iota(jnp.int32, (sample, rank), 0)
    odd = lax.broadcasted_iota(jnp.int32, (wide, 2 * rank), 0) % 2
    side = lax.broadcasted_iota(jnp.int32, (wide, 2 * rank), 1) // rank
    pieces = []
    for r in range(sample):
        line = jnp.sum(jnp.where(which == (r ^ my), four, 0.0), axis=0, keepdims=True)
        line = jnp.concatenate([line, line], axis=1)
        pieces.append(jnp.where(odd == side, line, 0.0))
    base_ref[...] = jnp.concatenate(pieces * 2, axis=0)
    row = (lax.broadcasted_iota(jnp.int32, base_ref.shape, 0) % wide) // 2

    def copy(b, slot, group):
        at = pl.multiple_of((first + b) * rank, rank)
        return pltpu.make_async_copy(
            ring.at[slot],
            out_hbm.at[pl.ds(group * each, each), pl.ds(at, rank)],
            sems.at[slot],
        )

    groups = rank // each

    def block(b):
        held = [
            part[pl.ds(pl.multiple_of((start + b) * times, 8), times), :] for part in parts
        ]
        joined = []
        for g in range(sample):
            joined += [h[:, g * wide : (g + 1) * wide] for h in held]
        high, low = split(jnp.concatenate(joined, axis=1))
        both = jnp.concatenate([high, low], axis=0)
        high, low = split(jnp.dot(three, both, preferred_element_type=F32))
        for g in range(sample):
            at = slice(g * rank, (g + 1) * rank)
            left_ref[at, :] = jnp.concatenate([high[:, at], low[:, at]], axis=1)

        def some(n, _):
            for slot in range(slots):
                group = n * slots + slot

                @pl.when((b > 0) | (n > 0))
                def _():
                    copy(0, slot, 0).wait()

                for m in range(span):
                    right = jnp.where(row == group * span + m, base_ref[...], 0.0).astype(BF16)
                    out = jnp.dot(left_ref[...], right, preferred_element_type=F32)
                    for g in range(sample):
                        for k in range(2):
                            ring[slot, m * 2 * sample + 2 * g + k] = out[
                                g * rank : (g + 1) * rank, k * rank : (k + 1) * rank
                            ]
                copy(b, slot, group).start()

        lax.fori_loop(0, groups // slots, some, None)

    pl.loop(0, count)(block)
    for slot in range(slots):
        copy(0, slot, 0).wait()


def final_core(parts, core_three, core_four, after, place, into):
    sample = len(parts)
    rank = core_three.shape[1]
    vmem, anywhere = pl.BlockSpec(memory_space=pltpu.VMEM), pl.BlockSpec(memory_space=pl.ANY)
    extra = list(after) + ([into] if into is not None else [])
    each = min(rank, 2 * sample * SPAN)
    slots = min(SLOTS, rank // each)
    return pl.pallas_call(
        functools.partial(final_kernel, sample, place),
        in_specs=[vmem] * (sample + 2) + [anywhere] * len(extra),
        out_specs=[anywhere, vmem],
        out_shape=[
            jax.ShapeDtypeStruct((rank, place[3] * rank, rank), F32),
            jax.ShapeDtypeStruct((8, 128), F32),
        ],
        scratch_shapes=[
            pltpu.VMEM((sample * rank, 2 * rank), BF16),
            pltpu.VMEM((2 * rank, 2 * rank), F32),
            pltpu.VMEM((slots, each, rank, rank), F32),
            pltpu.SemaphoreType.DMA((slots,)),
        ],
        input_output_aliases={sample + 1 + len(extra): 0} if into is not None else {},
        compiler_params=pltpu.CompilerParams(vmem_limit_bytes=32 * MIB),
        cost_estimate=LIGHT,
        name="final_core",
    )(*parts, core_three, core_four, *extra)


def swap(value, axis, mask):
    size = lax.axis_size(axis)
    return lax.ppermute(value, axis, [(i, i ^ mask) for i in range(size)])


def small_call(kernel, outs, name, args, after=()):
    vmem, anywhere = pl.BlockSpec(memory_space=pltpu.VMEM), pl.BlockSpec(memory_space=pl.ANY)
    count = len(args)

    def body(*refs):
        kernel(*refs[:count], *refs[count + len(after) :])

    return pl.pallas_call(
        body,
        in_specs=[vmem] * count + [anywhere] * len(after),
        out_specs=[vmem] * len(outs),
        out_shape=[jax.ShapeDtypeStruct(s, F32) for s in outs],
        compiler_params=pltpu.CompilerParams(vmem_limit_bytes=16 * MIB),
        cost_estimate=LIGHT,
        name=name,
    )(*args, *after)


def route(blocks, bit):
    stay = [u for u in blocks if not u & bit]
    return [u ^ bit for u in stay], stay


def core_kernel_add(rows, first, plans, *refs):
    ways = len(plans)
    ins, outs = refs[: 2 if first else 2 * ways], list(refs[2 if first else 2 * ways :])
    for way, (slots, bit) in enumerate(plans):
        stay, came = ins if first else ins[2 * way : 2 * way + 2]

        def total(n):
            u = slots[n]
            at = slice((u * ways + way) * rows, (u * ways + way + 1) * rows)
            if not first:
                at = slice(n * rows, (n + 1) * rows)
            return stay[at, :] + came[at, :]

        if bit:
            for chosen in route(slots, bit):
                out = outs.pop(0)
                for n, u in enumerate(chosen):
                    out[n * rows : (n + 1) * rows, :] = total(slots.index(u))
        else:
            value = total(0)
            each = outs[0].shape[0]
            for n in range(rows // each):
                outs.pop(0)[...] = value[n * each : (n + 1) * each]


def core_stage(values, plans, rows, first, sample, rank, after):
    ways = len(plans)
    shapes = []
    for slots, bit in plans:
        if bit:
            shapes += [(len(slots) // 2 * rows, rank)] * 2
        else:
            shapes += [(rows // (sample // ways), rank)] * (sample // ways)
    return small_call(
        functools.partial(core_kernel_add, rows, first, plans), shapes, "add_core", values, after
    )


def core_tree(space, sample):
    chips = space // 2
    bits = [1 << n for n in range(chips.bit_length() - 1)]
    ways = 2 if len(bits) > 1 and sample % 2 == 0 else 1
    orders = [bits[way:] + bits[:way] for way in range(ways)]
    held = [list(range(chips)) for _ in range(ways)]
    stages = []
    for n in range(len(bits) + 1):
        plans = []
        for way in range(ways):
            bit = orders[way][n] if n < len(bits) else 0
            plans.append((held[way], bit))
            if bit:
                held[way] = route(held[way], bit)[1]
        stages.append(plans)
    return stages


def add_kernel(blocks, rows, tail, *refs):
    keep_ref, got_ref, *outs = refs
    at = keep_ref.shape[0] - tail
    end = keep_ref[at:, :] + got_ref[at:, :]
    for u, out in zip(blocks, outs):
        at = slice(u * rows, (u + 1) * rows)
        out[:rows, :] = keep_ref[at, :] + got_ref[at, :]
        out[rows:, :] = end


def mix_kernel(sample, own, times, count, *refs):
    ins, first_ref, outs, fourth_ref = refs[:count], refs[count], refs[count + 1 : -1], refs[-1]
    total = ins[0][...]
    for ref in ins[1:]:
        total = total + ref[...]
    tail = sample * own
    third = total[tail : tail + times]
    for far in range(sample):
        outs[far][:own, :] = total[far * own : (far + 1) * own]
        outs[far][own : own + times, :] = third
        outs[far][own + times :, :] = first_ref[far]
    fourth_ref[...] = total[tail + times : tail + times + 1]


def end_kernel(sample, own, times, *refs):
    ins, (one_ref, two_ref, three_ref) = refs[:sample], refs[sample:]
    total = ins[0][...]
    for ref in ins[1:]:
        total = total + ref[...]
    two_ref[...] = total[:own]
    three_ref[...] = total[own : own + times]
    lines = total.shape[0] - own - times
    points = one_ref.shape[1]
    for n in range(one_ref.shape[0] // lines):
        one_ref[n * lines : (n + 1) * lines, :] = total[
            own + times :, n * points : (n + 1) * points
        ]


def on_device(
    ensemble, map_one, map_two, map_three, map_four, core_one, core_two, core_three, core_four
):
    space, sample = lax.axis_size("space"), lax.axis_size("sample")
    times, _, points, _ = ensemble.shape
    rank, width = core_two.shape[1], map_two.shape[1]
    chips = space // 2
    chunks = min(CHUNKS, rank // (space * sample))
    every = range(chunks)

    sent = core_partial(ensemble, core_one, core_two, space, sample, 8, chunks)
    keep, send = sent[:chunks], sent[chunks:]
    got = [swap(s, "space", 1) for s in send]
    stages = core_tree(space, sample)
    ways = len(stages[0])
    rows = keep[0].shape[0] // (chips * ways)
    state = [[keep[k], got[k]] for k in every]
    last = None
    for n, plans in enumerate(stages):
        for k in every:
            after = [] if last is None else [last]
            outs = core_stage(state[k], plans, rows, n == 0, sample, rank, after)
            last = outs[-1]
            if n + 1 < len(stages):
                state[k] = []
                for way, (_, bit) in enumerate(plans):
                    went, stayed = outs[2 * way : 2 * way + 2]
                    state[k] += [stayed, swap(went, "space", 2 * bit)]
            else:
                state[k] = [swap(p, "sample", far) if far else p for far, p in enumerate(outs)]
        if n == 0:
            mine, send, first = sketch_partial(
                ensemble, map_one, map_two, map_three, map_four, last, space, sample, 8
            )
            last = first
            theirs = swap(send, "space", 1)

    tail = times + 8
    lines = (mine.shape[0] - tail) // chips
    own = lines // sample
    near = [u for u in range(chips) if u & (u - 1) == 0]
    pieces = []
    for blocks, after in (
        (near, last),
        ([u for u in range(chips) if u not in near], state[-1][min(1, sample - 1)]),
    ):
        outs = small_call(
            functools.partial(add_kernel, blocks, lines, tail),
            [(lines + tail, width)] * len(blocks), "add_cores", [mine, theirs], [after],
        ) if blocks else []
        pieces += [swap(p, "space", 2 * u) if u else p for u, p in zip(blocks, outs)]

    total = rank // (space * sample)
    piece = total // chunks
    calls = [(k, 0, k * piece, piece) for k in every]
    if chunks == 1 and total > 1:
        calls = [(0, 0, 0, 1), (0, 1, 1, total - 1)]
    core, after = None, []
    for k, start, at, count in calls[:-1]:
        core, token = final_core(
            state[k], core_three, core_four, after, (start, at, count, total), core
        )
        after = [token]
    length = own + times + first.shape[1]
    *pieces, fourth = small_call(
        functools.partial(mix_kernel, sample, own, times, chips),
        [(length, width)] * sample + [(1, width)], "add_chips", [*pieces, first], after,
    )
    k, start, at, count = calls[-1]
    core, _ = final_core(
        state[k], core_three, core_four, [pieces[0]], (start, at, count, total), core
    )
    pieces = [swap(p, "sample", far) if far else p for far, p in enumerate(pieces)]
    one, two, three = small_call(
        functools.partial(end_kernel, sample, own, times),
        [(width // sample, points), (own, width), (times, width)], "add_samples", pieces,
    )
    return (one.T, two, three, fourth, core)


def solution(mesh):
    placed = (
        P(None, "sample", "space", None),
        P("space", None),
        P(),
        P(),
        P("sample", None),
        P(),
        P(),
        P(),
        P(),
    )
    return jax.shard_map(
        on_device,
        mesh=mesh,
        in_specs=placed,
        out_specs=(
            P("space", "sample"),
            P(("space", "sample"), None),
            P(),
            P("sample", None),
            P(None, ("space", "sample"), None),
        ),
        check_vma=False,
    )
```

profile of v0, /device:TPU:0, one launch (start us, length us, event | category | flops | bytes accessed | tf_op | source)
XLA Modules:
  0.0 70.7 jit_solution(207736439742497232)
XLA Ops:
  0.6 0.0 copy-start.1
  0.6 0.0 copy-start
  0.7 0.0 copy-start.3
  0.7 0.0 copy-start.5
  0.7 8.6 %core_partial.1 = (f32[3072,128]{1,0:T(8,128)S(1)}, f32[3072,128]{1,0:T(8,128)S(1)}) custom-call(bf16[48,1,128,1024]{3,2,1,0:T(8,128)(2,1)} %x_hbm.3, bf16[1024,128]{1,0:T(8,128)(2,1)} %two_hbm.1, bf16[1024,128]{1,0:T(8,128)(2,1)} %one_hbm.1), custom_call_target="tpu_custom_call" | custom-call | flops 1 | bytes 1 | tf_op jit(solution)/shard_map/core_partial/pallas_call | solution.py:97
  9.3 0.0 copy-start.2
  9.3 0.0 copy-start.4
  9.3 0.5 collective-permute-start
  9.8 3.0 %collective-permute-done.refs_1_ = f32[3072,128]{1,0:T(8,128)S(1)} collective-permute-done((f32[3072,128]{1,0:T(8,128)S(1)}, f32[3072,128]{1,0:T(8,128)S(1)}, u32[]{:S(2)}, u32[]{:S(2)}) %collective-permute-start) | collective-permute-done | bytes 1572896 | tf_op jit(solution)/shard_map/ppermute | solution.py:344
  12.8 0.2 add_core.3
  13.0 2.9 %collective-permute-start.2 = (f32[768,128]{1,0:T(8,128)S(1)}, f32[768,128]{1,0:T(8,128)S(1)}, u32[]{:S(2)}, u32[]{:S(2)}) collective-permute-start(f32[768,128]{1,0:T(8,128)S(1)} %get-tuple-element.42), channel_id=1, source_target_pairs={{0,8},{4,12},{8,0},{12,4},{16,24},{20,28},{24,16},{28,20},{1,9},{5... | collective-permute-start | bytes 1179656 | tf_op jit(solution)/shard_map/ppermute | solution.py:344
  15.9 1.5 %collective-permute-start.3 = (f32[768,128]{1,0:T(8,128)S(1)}, f32[768,128]{1,0:T(8,128)S(1)}, u32[]{:S(2)}, u32[]{:S(2)}) collective-permute-start(f32[768,128]{1,0:T(8,128)S(1)} %get-tuple-element.43), channel_id=1, source_target_pairs={{0,16},{4,20},{8,24},{12,28},{16,0},{20,4},{24,8},{28,12},{1,17},{... | collective-permute-start | bytes 1179656 | tf_op jit(solution)/shard_map/ppermute | solution.py:344
  17.5 0.0 copy-done.1
  17.5 0.0 copy-done
  17.5 0.0 copy-done.5
  17.5 9.9 %sketch_partial.1 = (f32[568,256]{1,0:T(8,128)S(1)}, f32[568,256]{1,0:T(8,128)S(1)}, f32[4,32,256]{2,1,0:T(8,128)S(1)}) custom-call(bf16[48,1,128,1024]{3,2,1,0:T(8,128)(2,1)} %x_hbm.3, bf16[128,256]{1,0:T(8,128)(2,1)S(1)} %copy-done.1, bf16[1024,256]{1,0:T(8,128)(2,1)S(1)} %copy-done, bf16[48,256]{1,0:T(8,128)(2,1)S(1)} %copy-done.3, ...), custom_call_target="tpu_custom_call" | custom-call | flops 1 | bytes 1 | tf_op jit(solution)/shard_map/sketch_partial/pallas_call | solution.py:211
  27.3 0.1 collective-permute-start.1
  27.4 0.0 collective-permute-done.2.refs_1_
  27.4 0.0 collective-permute-done.3.refs_3_
  27.4 0.1 add_core.4
  27.5 0.9 %collective-permute-start.4 = (f32[384,128]{1,0:T(8,128)S(1)}, f32[384,128]{1,0:T(8,128)S(1)}, u32[]{:S(2)}, u32[]{:S(2)}) collective-permute-start(f32[384,128]{1,0:T(8,128)S(1)} %get-tuple-element.46), channel_id=1, source_target_pairs={{0,16},{4,20},{8,24},{12,28},{16,0},{20,4},{24,8},{28,12},{1,17},{... | collective-permute-start | bytes 589832 | tf_op jit(solution)/shard_map/ppermute | solution.py:344
  28.5 0.5 collective-permute-start.5
  29.0 5.9 %collective-permute-done.4.refs_1_ = f32[384,128]{1,0:T(8,128)S(1)} collective-permute-done((f32[384,128]{1,0:T(8,128)S(1)}, f32[384,128]{1,0:T(8,128)S(1)}, u32[]{:S(2)}, u32[]{:S(2)}) %collective-permute-start.4) | collective-permute-done | bytes 196640 | tf_op jit(solution)/shard_map/ppermute | solution.py:344
  34.9 0.2 collective-permute-done.5.refs_3_
  35.2 1.7 %collective-permute-start.8 = (f32[192,128]{1,0:T(8,128)S(1)}, f32[192,128]{1,0:T(8,128)S(1)}, u32[]{:S(2)}, u32[]{:S(2)}) collective-permute-start(f32[192,128]{1,0:T(8,128)S(1)} %get-tuple-element.53), channel_id=1, source_target_pairs={{0,1},{1,0},{2,3},{3,2},{4,5},{5,4},{6,7},{7,6},{8,9},{9,8},{10,11... | collective-permute-start | bytes 294920 | tf_op jit(solution)/shard_map/ppermute | solution.py:344
  36.8 0.0 collective-permute-done.1.refs_1_
  36.8 0.1 add_cores.2
  36.9 0.6 collective-permute-start.6
  37.5 1.5 %collective-permute-start.7 = (f32[184,256]{1,0:T(8,128)S(1)}, f32[184,256]{1,0:T(8,128)S(1)}, u32[]{:S(2)}, u32[]{:S(2)}) collective-permute-start(f32[184,256]{1,0:T(8,128)S(1)} %get-tuple-element.52), channel_id=1, source_target_pairs={{0,16},{4,20},{8,24},{12,28},{16,0},{20,4},{24,8},{28,12},{1,17},{... | collective-permute-start | bytes 565256 | tf_op jit(solution)/shard_map/ppermute | solution.py:344
  39.0 0.8 %collective-permute-done.8.refs_2_.refs_1_ = f32[192,128]{1,0:T(8,128)S(1)} collective-permute-done((f32[192,128]{1,0:T(8,128)S(1)}, f32[192,128]{1,0:T(8,128)S(1)}, u32[]{:S(2)}, u32[]{:S(2)}) %collective-permute-start.8) | collective-permute-done | bytes 98336 | tf_op jit(solution)/shard_map/ppermute | solution.py:344
  39.9 1.6 %collective-permute-start.9 = (f32[184,256]{1,0:T(8,128)S(1)}, f32[184,256]{1,0:T(8,128)S(1)}, u32[]{:S(2)}, u32[]{:S(2)}) collective-permute-start(f32[184,256]{1,0:T(8,128)S(1)} %add_cores.3), channel_id=1, source_target_pairs={{0,24},{4,28},{8,16},{12,20},{16,8},{20,12},{24,0},{28,4},{1,25},{... | collective-permute-start | bytes 565256 | tf_op jit(solution)/shard_map/ppermute | solution.py:344
  41.4 2.6 %collective-permute-start.10 = (f32[192,128]{1,0:T(8,128)S(1)}, f32[192,128]{1,0:T(8,128)S(1)}, u32[]{:S(2)}, u32[]{:S(2)}) collective-permute-start(f32[192,128]{1,0:T(8,128)S(1)} %get-tuple-element.55), channel_id=1, source_target_pairs={{0,2},{1,3},{2,0},{3,1},{4,6},{5,7},{6,4},{7,5},{8,10},{9,11},{10,... | collective-permute-start | bytes 294920 | tf_op jit(solution)/shard_map/ppermute | solution.py:344
  44.0 1.4 %collective-permute-start.11 = (f32[192,128]{1,0:T(8,128)S(1)}, f32[192,128]{1,0:T(8,128)S(1)}, u32[]{:S(2)}, u32[]{:S(2)}) collective-permute-start(f32[192,128]{1,0:T(8,128)S(1)} %get-tuple-element.49.refs_2_), channel_id=1, source_target_pairs={{0,3},{1,2},{2,1},{3,0},{4,7},{5,6},{6,5},{7,4},{8,11},{9,10},{10,... | collective-permute-start | bytes 294920 | tf_op jit(solution)/shard_map/ppermute | solution.py:344
  45.4 5.2 %collective-permute-done.10.refs_2_ = f32[192,128]{1,0:T(8,128)S(1)} collective-permute-done((f32[192,128]{1,0:T(8,128)S(1)}, f32[192,128]{1,0:T(8,128)S(1)}, u32[]{:S(2)}, u32[]{:S(2)}) %collective-permute-start.10) | collective-permute-done | bytes 98336 | tf_op jit(solution)/shard_map/ppermute | solution.py:344
  50.6 0.0 collective-permute-done.11.refs_3_
  50.6 4.0 %final_core.2 = (f32[128,512,128]{2,1,0:T(8,128)}, f32[8,128]{1,0:T(8,128)S(1)}) custom-call(f32[192,128]{1,0:T(8,128)S(1)} %get-tuple-element.54.refs_0_, f32[192,128]{1,0:T(8,128)S(1)} %collective-permute-done.8.refs_2_.refs_1_, f32[192,128]{1,0:T(8,128)S(1)} %collective-permute-done.10.refs_2_, f32[192,128]{1,0:T(8,128)S(1)} %collective-permute-done.11.refs_3_, ...), custom_call_target="tpu_custom_call" | custom-call | flops 1 | bytes 1 | tf_op jit(solution)/shard_map/final_core/pallas_call | solution.py:321
  54.6 0.0 collective-permute-done.6.refs_1_
  54.6 0.0 collective-permute-done.7.refs_2_
  54.6 0.0 collective-permute-done.9.refs_3_
  54.6 0.6 add_chips.1
  55.3 1.6 %collective-permute-start.12 = (f32[112,256]{1,0:T(8,128)S(1)}, f32[112,256]{1,0:T(8,128)S(1)}, u32[]{:S(2)}, u32[]{:S(2)}) collective-permute-start(f32[112,256]{1,0:T(8,128)S(1)} %get-tuple-element.58), channel_id=1, source_target_pairs={{0,1},{1,0},{2,3},{3,2},{4,5},{5,4},{6,7},{7,6},{8,9},{9,8},{10,11... | collective-permute-start | bytes 344072 | tf_op jit(solution)/shard_map/ppermute | solution.py:344
  56.9 2.1 %collective-permute-start.13 = (f32[112,256]{1,0:T(8,128)S(1)}, f32[112,256]{1,0:T(8,128)S(1)}, u32[]{:S(2)}, u32[]{:S(2)}) collective-permute-start(f32[112,256]{1,0:T(8,128)S(1)} %get-tuple-element.59), channel_id=1, source_target_pairs={{0,2},{1,3},{2,0},{3,1},{4,6},{5,7},{6,4},{7,5},{8,10},{9,11},{10,... | collective-permute-start | bytes 344072 | tf_op jit(solution)/shard_map/ppermute | solution.py:344
  59.0 1.0 %collective-permute-start.14 = (f32[112,256]{1,0:T(8,128)S(1)}, f32[112,256]{1,0:T(8,128)S(1)}, u32[]{:S(2)}, u32[]{:S(2)}) collective-permute-start(f32[112,256]{1,0:T(8,128)S(1)} %get-tuple-element.60), channel_id=1, source_target_pairs={{0,3},{1,2},{2,1},{3,0},{4,7},{5,6},{6,5},{7,4},{8,11},{9,10},{10,... | collective-permute-start | bytes 344072 | tf_op jit(solution)/shard_map/ppermute | solution.py:344
  60.0 9.9 %final_core.3 = (f32[128,512,128]{2,1,0:T(8,128)}, f32[8,128]{1,0:T(8,128)}) custom-call(f32[192,128]{1,0:T(8,128)S(1)} %get-tuple-element.54.refs_0_, f32[192,128]{1,0:T(8,128)S(1)} %collective-permute-done.8.refs_2_.refs_1_, f32[192,128]{1,0:T(8,128)S(1)} %collective-permute-done.10.refs_2_, ...), custom_call_target="tpu_custom_call", output_to_operand_aliasing={{0}: (7, {})} | custom-call | flops 1 | bytes 1 | tf_op jit(solution)/shard_map/final_core/pallas_call | solution.py:321
  70.0 0.0 collective-permute-done.12.refs_1_
  70.0 0.0 collective-permute-done.13.refs_2_
  70.0 0.0 collective-permute-done.14.refs_3_
  70.0 0.7 add_samples.1
  (5 shorter events, 0.1 us)
Async XLA Ops:
  0.6 16.8 %copy-start.1 = (bf16[128,256]{1,0:T(8,128)(2,1)S(1)}, bf16[128,256]{1,0:T(8,128)(2,1)}, u32[]{:S(2)}) copy-start(bf16[128,256]{1,0:T(8,128)(2,1)} %one_ref.1) | copy-start | bytes 196612
  0.6 16.8 %copy-start = (bf16[1024,256]{1,0:T(8,128)(2,1)S(1)}, bf16[1024,256]{1,0:T(8,128)(2,1)}, u32[]{:S(2)}) copy-start(bf16[1024,256]{1,0:T(8,128)(2,1)} %two_ref.1) | copy-start | bytes 1572868
  0.7 16.8 %copy-start.3 = (bf16[48,256]{1,0:T(8,128)(2,1)S(1)}, bf16[48,256]{1,0:T(8,128)(2,1)}, u32[]{:S(2)}) copy-start(bf16[48,256]{1,0:T(8,128)(2,1)} %three_ref.1) | copy-start | bytes 73732
  0.7 16.8 %copy-start.5 = (bf16[1,256]{1,0:T(2,128)(2,1)S(1)}, bf16[1,256]{1,0:T(2,128)(2,1)}, u32[]{:S(2)}) copy-start(bf16[1,256]{1,0:T(2,128)(2,1)} %four_ref.1) | copy-start | bytes 1540
  9.3 41.3 %copy-start.2 = (bf16[48,128]{1,0:T(8,128)(2,1)S(1)}, bf16[48,128]{1,0:T(8,128)(2,1)}, u32[]{:S(2)}) copy-start(bf16[48,128]{1,0:T(8,128)(2,1)} %refs_4_.3) | copy-start | bytes 36868
  9.3 41.3 %copy-start.4 = (bf16[4,128]{1,0:T(4,128)(2,1)S(1)}, bf16[4,128]{1,0:T(4,128)(2,1)}, u32[]{:S(2)}) copy-start(bf16[4,128]{1,0:T(4,128)(2,1)} %refs_5_.3) | copy-start | bytes 3076
  9.3 3.5 %collective-permute-start = (f32[3072,128]{1,0:T(8,128)S(1)}, f32[3072,128]{1,0:T(8,128)S(1)}, u32[]{:S(2)}, u32[]{:S(2)}) collective-permute-start(f32[3072,128]{1,0:T(8,128)S(1)} %get-tuple-element.37), channel_id=1, source_target_pairs={{0,4},{4,0},{8,12},{12,8},{16,20},{20,16},{24,28},{28,24},{1,5},{5... | collective-permute-start | bytes 4718600 | tf_op jit(solution)/shard_map/ppermute | solution.py:344
  13.0 14.4 %collective-permute-start.2 = (f32[768,128]{1,0:T(8,128)S(1)}, f32[768,128]{1,0:T(8,128)S(1)}, u32[]{:S(2)}, u32[]{:S(2)}) collective-permute-start(f32[768,128]{1,0:T(8,128)S(1)} %get-tuple-element.42), channel_id=1, source_target_pairs={{0,8},{4,12},{8,0},{12,4},{16,24},{20,28},{24,16},{28,20},{1,9},{5... | collective-permute-start | bytes 1179656 | tf_op jit(solution)/shard_map/ppermute | solution.py:344
  15.9 11.5 %collective-permute-start.3 = (f32[768,128]{1,0:T(8,128)S(1)}, f32[768,128]{1,0:T(8,128)S(1)}, u32[]{:S(2)}, u32[]{:S(2)}) collective-permute-start(f32[768,128]{1,0:T(8,128)S(1)} %get-tuple-element.43), channel_id=1, source_target_pairs={{0,16},{4,20},{8,24},{12,28},{16,0},{20,4},{24,8},{28,12},{1,17},{... | collective-permute-start | bytes 1179656 | tf_op jit(solution)/shard_map/ppermute | solution.py:344
  27.3 9.5 %collective-permute-start.1 = (f32[568,256]{1,0:T(8,128)S(1)}, f32[568,256]{1,0:T(8,128)S(1)}, u32[]{:S(2)}, u32[]{:S(2)}) collective-permute-start(f32[568,256]{1,0:T(8,128)S(1)} %get-tuple-element.40), channel_id=1, source_target_pairs={{0,4},{4,0},{8,12},{12,8},{16,20},{20,16},{24,28},{28,24},{1,5},{5... | collective-permute-start | bytes 1744904 | tf_op jit(solution)/shard_map/ppermute | solution.py:344
  27.5 7.3 %collective-permute-start.4 = (f32[384,128]{1,0:T(8,128)S(1)}, f32[384,128]{1,0:T(8,128)S(1)}, u32[]{:S(2)}, u32[]{:S(2)}) collective-permute-start(f32[384,128]{1,0:T(8,128)S(1)} %get-tuple-element.46), channel_id=1, source_target_pairs={{0,16},{4,20},{8,24},{12,28},{16,0},{20,4},{24,8},{28,12},{1,17},{... | collective-permute-start | bytes 589832 | tf_op jit(solution)/shard_map/ppermute | solution.py:344
  28.5 6.6 %collective-permute-start.5 = (f32[384,128]{1,0:T(8,128)S(1)}, f32[384,128]{1,0:T(8,128)S(1)}, u32[]{:S(2)}, u32[]{:S(2)}) collective-permute-start(f32[384,128]{1,0:T(8,128)S(1)} %get-tuple-element.48), channel_id=1, source_target_pairs={{0,8},{4,12},{8,0},{12,4},{16,24},{20,28},{24,16},{28,20},{1,9},{5... | collective-permute-start | bytes 589832 | tf_op jit(solution)/shard_map/ppermute | solution.py:344
  35.2 4.7 %collective-permute-start.8 = (f32[192,128]{1,0:T(8,128)S(1)}, f32[192,128]{1,0:T(8,128)S(1)}, u32[]{:S(2)}, u32[]{:S(2)}) collective-permute-start(f32[192,128]{1,0:T(8,128)S(1)} %get-tuple-element.53), channel_id=1, source_target_pairs={{0,1},{1,0},{2,3},{3,2},{4,5},{5,4},{6,7},{7,6},{8,9},{9,8},{10,11... | collective-permute-start | bytes 294920 | tf_op jit(solution)/shard_map/ppermute | solution.py:344
  36.9 17.7 %collective-permute-start.6 = (f32[184,256]{1,0:T(8,128)S(1)}, f32[184,256]{1,0:T(8,128)S(1)}, u32[]{:S(2)}, u32[]{:S(2)}) collective-permute-start(f32[184,256]{1,0:T(8,128)S(1)} %get-tuple-element.51), channel_id=1, source_target_pairs={{0,8},{4,12},{8,0},{12,4},{16,24},{20,28},{24,16},{28,20},{1,9},{5... | collective-permute-start | bytes 565256 | tf_op jit(solution)/shard_map/ppermute | solution.py:344
  37.5 17.1 %collective-permute-start.7 = (f32[184,256]{1,0:T(8,128)S(1)}, f32[184,256]{1,0:T(8,128)S(1)}, u32[]{:S(2)}, u32[]{:S(2)}) collective-permute-start(f32[184,256]{1,0:T(8,128)S(1)} %get-tuple-element.52), channel_id=1, source_target_pairs={{0,16},{4,20},{8,24},{12,28},{16,0},{20,4},{24,8},{28,12},{1,17},{... | collective-permute-start | bytes 565256 | tf_op jit(solution)/shard_map/ppermute | solution.py:344
  39.9 14.8 %collective-permute-start.9 = (f32[184,256]{1,0:T(8,128)S(1)}, f32[184,256]{1,0:T(8,128)S(1)}, u32[]{:S(2)}, u32[]{:S(2)}) collective-permute-start(f32[184,256]{1,0:T(8,128)S(1)} %add_cores.3), channel_id=1, source_target_pairs={{0,24},{4,28},{8,16},{12,20},{16,8},{20,12},{24,0},{28,4},{1,25},{... | collective-permute-start | bytes 565256 | tf_op jit(solution)/shard_map/ppermute | solution.py:344
  41.4 9.1 %collective-permute-start.10 = (f32[192,128]{1,0:T(8,128)S(1)}, f32[192,128]{1,0:T(8,128)S(1)}, u32[]{:S(2)}, u32[]{:S(2)}) collective-permute-start(f32[192,128]{1,0:T(8,128)S(1)} %get-tuple-element.55), channel_id=1, source_target_pairs={{0,2},{1,3},{2,0},{3,1},{4,6},{5,7},{6,4},{7,5},{8,10},{9,11},{10,... | collective-permute-start | bytes 294920 | tf_op jit(solution)/shard_map/ppermute | solution.py:344
  44.0 6.5 %collective-permute-start.11 = (f32[192,128]{1,0:T(8,128)S(1)}, f32[192,128]{1,0:T(8,128)S(1)}, u32[]{:S(2)}, u32[]{:S(2)}) collective-permute-start(f32[192,128]{1,0:T(8,128)S(1)} %get-tuple-element.49.refs_2_), channel_id=1, source_target_pairs={{0,3},{1,2},{2,1},{3,0},{4,7},{5,6},{6,5},{7,4},{8,11},{9,10},{10,... | collective-permute-start | bytes 294920 | tf_op jit(solution)/shard_map/ppermute | solution.py:344
  55.3 14.7 %collective-permute-start.12 = (f32[112,256]{1,0:T(8,128)S(1)}, f32[112,256]{1,0:T(8,128)S(1)}, u32[]{:S(2)}, u32[]{:S(2)}) collective-permute-start(f32[112,256]{1,0:T(8,128)S(1)} %get-tuple-element.58), channel_id=1, source_target_pairs={{0,1},{1,0},{2,3},{3,2},{4,5},{5,4},{6,7},{7,6},{8,9},{9,8},{10,11... | collective-permute-start | bytes 344072 | tf_op jit(solution)/shard_map/ppermute | solution.py:344
  56.9 13.1 %collective-permute-start.13 = (f32[112,256]{1,0:T(8,128)S(1)}, f32[112,256]{1,0:T(8,128)S(1)}, u32[]{:S(2)}, u32[]{:S(2)}) collective-permute-start(f32[112,256]{1,0:T(8,128)S(1)} %get-tuple-element.59), channel_id=1, source_target_pairs={{0,2},{1,3},{2,0},{3,1},{4,6},{5,7},{6,4},{7,5},{8,10},{9,11},{10,... | collective-permute-start | bytes 344072 | tf_op jit(solution)/shard_map/ppermute | solution.py:344
  59.0 11.0 %collective-permute-start.14 = (f32[112,256]{1,0:T(8,128)S(1)}, f32[112,256]{1,0:T(8,128)S(1)}, u32[]{:S(2)}, u32[]{:S(2)}) collective-permute-start(f32[112,256]{1,0:T(8,128)S(1)} %get-tuple-element.60), channel_id=1, source_target_pairs={{0,3},{1,2},{2,1},{3,0},{4,7},{5,6},{6,5},{7,4},{8,11},{9,10},{10,... | collective-permute-start | bytes 344072 | tf_op jit(solution)/shard_map/ppermute | solution.py:344
where the time goes:
time: 70.8 us; the launch traced here: 70.7 us
  Pallas kernels  34.1 us (48%)
  starting transfers between devices  20.6 us (29%)
  waiting for transfers between devices  15.2 us (21%)
  between operations  0.82 us (1%)
    ppermute x15, starting transfers between devices, swap(): return lax.ppermute(value, axis, [(i, i ^ mask) for i in range(size)])  20.6 us
    ppermute x15, waiting for transfers between devices, swap(): return lax.ppermute(value, axis, [(i, i ^ mask) for i in range(size)])  15.2 us
    pallas_call x2, Pallas kernels, final_core(): pl.pallas_call(functools.partial(final_kernel, sample, place), in_specs=[...  13.9 us
    pallas_call x1, Pallas kernels, sketch_partial(): pl.pallas_call(functools.partial(sketch_kernel, space, sample, block), in...  9.87 us
    pallas_call x1, Pallas kernels, core_partial(): pl.pallas_call(functools.partial(core_kernel, space, sample, block, chunk...  8.59 us
    pallas_call x7, Pallas kernels, small_call(): pl.pallas_call(body, in_specs=[vmem] * count + [anywhere] * len(after), o...  1.7 us
  transfers between devices with their start and end apart: 15, of which 5 were waited for; matrix products, arithmetic and copies ran while one was open for 0% of the time, Pallas kernels for 34%

commit v1 on v0

--- a/solution.py
+++ b/solution.py
@@ -12,6 +12,7 @@
 NT = (((1,), (1,)), ((), ()))
 MIB = 1 << 20
 CHUNKS = 1
+BLOCK, PORTIONS = 4, (2, 4, 6)
 SPAN, SLOTS = 4, 4
 LIGHT = pl.CostEstimate(flops=1, bytes_accessed=1, transcendentals=0)
 
@@ -19,6 +20,13 @@
 def split(value):
     high = value.astype(BF16)
     return high, (value - high.astype(F32)).astype(BF16)
+
+
+def portions(times, block):
+    lengths = [n * block for n in PORTIONS]
+    while sum(lengths) < times:
+        lengths.append(min(lengths[-1], times - sum(lengths)))
+    return lengths
 
 
 def core_kernel(
@@ -71,22 +79,25 @@
     ordered = jnp.dot(one_ref[...], order, preferred_element_type=F32).astype(BF16)
     right_ref[...] = jnp.concatenate([ordered, ordered], axis=0)
 
-    for n in range(count):
-        loads[n].wait()
-        x = x_ref[n * block : (n + 1) * block].reshape(block * points, x_ref.shape[2])
+    size = half // chunks
+    start = 0
+    for length in portions(times, block):
+        for n in range(start // block, (start + length) // block):
+            loads[n].wait()
+        x = x_ref[start : start + length].reshape(length * points, x_ref.shape[2])
         first = lax.dot_general(left_ref[...], x, NT, preferred_element_type=F32)
         rows = []
-        for t in range(block):
+        for t in range(length):
             high, low = split(first[:, t * points : (t + 1) * points])
             rows.append(jnp.concatenate([high, low], axis=1))
         out = jnp.dot(
             jnp.concatenate(rows, axis=0), right_ref[...], preferred_element_type=F32
         )
-        size = half // chunks
-        for t in range(block):
+        for t in range(length):
             for k in range(2 * chunks):
                 at = t * rank + k * size
-                outs[k][pl.ds(n * block + t, size, stride=times), :] = out[at : at + size]
+                outs[k][pl.ds(start + t, size, stride=times), :] = out[at : at + size]
+        start += length
 
 
 def core_partial(ensemble, core_one, core_two, space, sample, block, chunks):
@@ -120,7 +131,7 @@
 def sketch_kernel(
     space, sample, block, x_hbm, one_ref, two_ref, three_ref, four_ref, after_ref,
     keep_ref, send_ref, first_ref,
-    x_ref, acc_one, acc_two, acc_u, pairs, rolled, one_t, turned, sems,
+    x_ref, acc_one, acc_two, acc_u, pairs, flipped, one_t, turned, sems,
 ):
     del after_ref
     times, points, cols = x_ref.shape
@@ -134,38 +145,35 @@
     ]
     for load in loads:
         load.start()
-    acc_one[...] = jnp.zeros_like(acc_one)
-    acc_two[...] = jnp.zeros_like(acc_two)
     four = four_ref[...].astype(F32)
     pair = three_ref[...].astype(F32) * four
-    pairs[...] = pair.reshape(pairs.shape)
+    pairs[...] = pair
     padded = jnp.concatenate([pair, jnp.zeros((128 - times, width), F32)], axis=0)
-    flipped = padded.T
-    for n in range(count):
-        rolled[n] = pltpu.roll(flipped, (128 - n * block) % 128, 1)
+    flipped[...] = padded.T
     one = one_ref[...].astype(F32)
     if points < 128:
         one = jnp.concatenate([one, jnp.zeros((128 - points, width), F32)], axis=0)
     one_t[...] = one.T[:, :points]
 
-    for step in range(count):
-        loads[step].wait()
-        x = x_ref[step * block : (step + 1) * block].reshape(block * points, cols)
+    start = 0
+    for length in portions(times, block):
+        for n in range(start // block, (start + length) // block):
+            loads[n].wait()
+        x = x_ref[start : start + length].reshape(length * points, cols)
         proj = jnp.dot(x, two_ref[...], preferred_element_type=F32)
         one = one_ref[...].astype(F32)
-        weights = rolled[step]
-        total = acc_one[...]
-        sums, krao = [], []
-        for t in range(block):
+        total = acc_one[...] if start else jnp.zeros_like(acc_one)
+        krao = []
+        for t in range(length):
+            at = start + t
             part = proj[t * points : (t + 1) * points]
-            total = total + part * pairs[step, t : t + 1, :]
-            sums.append(jnp.sum(part * one, axis=0, keepdims=True))
-            krao.append((weights[:, t : t + 1] * one_t[...]).astype(BF16))
+            total = total + part * pairs[at : at + 1, :]
+            acc_u[at : at + 1, :] = jnp.sum(part * one, axis=0, keepdims=True)
+            krao.append((flipped[:, at : at + 1] * one_t[...]).astype(BF16))
         acc_one[...] = total
-        acc_u[step] = jnp.concatenate(sums, axis=0)
-        acc_two[...] += jnp.dot(
-            jnp.concatenate(krao, axis=1), x, preferred_element_type=F32
-        )
+        more = jnp.dot(jnp.concatenate(krao, axis=1), x, preferred_element_type=F32)
+        acc_two[...] = acc_two[...] + more if start else more
+        start += length
 
     me, my = lax.axis_index("space"), lax.axis_index("sample")
     turned[...] = acc_two[...].T
@@ -176,7 +184,7 @@
             place = (slot ^ me) * sample + (far ^ my)
             at = (slot // 2 * sample + far) * own
             ref[at : at + own, :] = turned[pl.ds(pl.multiple_of(place * own, own), own), :]
-    u = acc_u[...].reshape(times, width)
+    u = acc_u[...]
     three = three_ref[...].astype(F32)
     tail = space // 2 * sample * own
     third = u * four_ref[...].astype(F32)
@@ -219,9 +227,9 @@
             pltpu.VMEM((times, points, cols), BF16),
             pltpu.VMEM((points, width), F32),
             pltpu.VMEM((width, cols), F32),
-            pltpu.VMEM((times // block, block, width), F32),
-            pltpu.VMEM((times // block, block, width), F32),
-            pltpu.VMEM((times // block, width, 128), F32),
+            pltpu.VMEM((times, width), F32),
+            pltpu.VMEM((times, width), F32),
+            pltpu.VMEM((width, 128), F32),
             pltpu.VMEM((width, points), F32),
             pltpu.VMEM((cols, width), F32),
             pltpu.SemaphoreType.DMA((times // block,)),
@@ -334,7 +342,9 @@
         ],
         input_output_aliases={sample + 1 + len(extra): 0} if into is not None else {},
         compiler_params=pltpu.CompilerParams(vmem_limit_bytes=32 * MIB),
-        cost_estimate=LIGHT,
+        cost_estimate=pl.CostEstimate(
+            flops=4 * rank**4, bytes_accessed=4 * place[2] * rank**3, transcendentals=0
+        ),
         name="final_core",
     )(*parts, core_three, core_four, *extra)
 
@@ -367,9 +377,13 @@
     return [u ^ bit for u in stay], stay
 
 
-def core_kernel_add(rows, first, plans, *refs):
+def core_kernel_add(rows, first, plans, passed, *refs):
     ways = len(plans)
-    ins, outs = refs[: 2 if first else 2 * ways], list(refs[2 if first else 2 * ways :])
+    count = 2 if first else 2 * ways
+    ins, outs = refs[:count], list(refs[count:])
+    if passed:
+        outs[-1][...] = outs[0][...]
+        outs = outs[1:-1]
     for way, (slots, bit) in enumerate(plans):
         stay, came = ins if first else ins[2 * way : 2 * way + 2]
 
@@ -392,7 +406,7 @@
                 outs.pop(0)[...] = value[n * each : (n + 1) * each]
 
 
-def core_stage(values, plans, rows, first, sample, rank, after):
+def core_stage(values, plans, rows, first, sample, rank, after, passed=None):
     ways = len(plans)
     shapes = []
     for slots, bit in plans:
@@ -400,8 +414,11 @@
             shapes += [(len(slots) // 2 * rows, rank)] * 2
         else:
             shapes += [(rows // (sample // ways), rank)] * (sample // ways)
+    if passed is not None:
+        values, shapes = [*values, passed], [*shapes, passed.shape]
     return small_call(
-        functools.partial(core_kernel_add, rows, first, plans), shapes, "add_core", values, after
+        functools.partial(core_kernel_add, rows, first, plans, passed is not None),
+        shapes, "add_core", values, after,
     )
 
 
@@ -472,7 +489,7 @@
     chunks = min(CHUNKS, rank // (space * sample))
     every = range(chunks)
 
-    sent = core_partial(ensemble, core_one, core_two, space, sample, 8, chunks)
+    sent = core_partial(ensemble, core_one, core_two, space, sample, BLOCK, chunks)
     keep, send = sent[:chunks], sent[chunks:]
     got = [swap(s, "space", 1) for s in send]
     stages = core_tree(space, sample)
@@ -483,7 +500,10 @@
     for n, plans in enumerate(stages):
         for k in every:
             after = [] if last is None else [last]
-            outs = core_stage(state[k], plans, rows, n == 0, sample, rank, after)
+            passed = send if n == 1 and k == chunks - 1 else None
+            outs = core_stage(state[k], plans, rows, n == 0, sample, rank, after, passed)
+            if passed is not None:
+                *outs, send = outs
             last = outs[-1]
             if n + 1 < len(stages):
                 state[k] = []
@@ -494,46 +514,33 @@
                 state[k] = [swap(p, "sample", far) if far else p for far, p in enumerate(outs)]
         if n == 0:
             mine, send, first = sketch_partial(
-                ensemble, map_one, map_two, map_three, map_four, last, space, sample, 8
+                ensemble, map_one, map_two, map_three, map_four, last, space, sample, BLOCK
             )
             last = first
+        if n == min(1, len(stages) - 1):
             theirs = swap(send, "space", 1)
-
-    tail = times + 8
-    lines = (mine.shape[0] - tail) // chips
-    own = lines // sample
-    near = [u for u in range(chips) if u & (u - 1) == 0]
-    pieces = []
-    for blocks, after in (
-        (near, last),
-        ([u for u in range(chips) if u not in near], state[-1][min(1, sample - 1)]),
-    ):
-        outs = small_call(
-            functools.partial(add_kernel, blocks, lines, tail),
-            [(lines + tail, width)] * len(blocks), "add_cores", [mine, theirs], [after],
-        ) if blocks else []
-        pieces += [swap(p, "space", 2 * u) if u else p for u, p in zip(blocks, outs)]
+            tail = times + 8
+            lines = (mine.shape[0] - tail) // chips
+            own = lines // sample
+            pieces = small_call(
+                functools.partial(add_kernel, list(range(chips)), lines, tail),
+                [(lines + tail, width)] * chips, "add_cores", [mine, theirs], [last],
+            )
+            last = pieces[0]
+            pieces = [swap(p, "space", 2 * u) if u else p for u, p in enumerate(pieces)]
 
     total = rank // (space * sample)
     piece = total // chunks
-    calls = [(k, 0, k * piece, piece) for k in every]
-    if chunks == 1 and total > 1:
-        calls = [(0, 0, 0, 1), (0, 1, 1, total - 1)]
-    core, after = None, []
-    for k, start, at, count in calls[:-1]:
-        core, token = final_core(
-            state[k], core_three, core_four, after, (start, at, count, total), core
-        )
-        after = [token]
     length = own + times + first.shape[1]
     *pieces, fourth = small_call(
         functools.partial(mix_kernel, sample, own, times, chips),
-        [(length, width)] * sample + [(1, width)], "add_chips", [*pieces, first], after,
-    )
-    k, start, at, count = calls[-1]
-    core, _ = final_core(
-        state[k], core_three, core_four, [pieces[0]], (start, at, count, total), core
-    )
+        [(length, width)] * sample + [(1, width)], "add_chips", [*pieces, first],
+    )
+    core = None
+    for k in every:
+        core, _ = final_core(
+            state[k], core_three, core_four, [pieces[0]], (0, k * piece, piece, total), core
+        )
     pieces = [swap(p, "sample", far) if far else p for far, p in enumerate(pieces)]
     one, two, three = small_call(
         functools.partial(end_kernel, sample, own, times),

time: 70.8 us -> 61.5 us (0.87)
  waiting for transfers between devices: 15.2 us -> 6.6 us
  Pallas kernels: 34.1 us -> 31.7 us
  starting transfers between devices: 20.6 us -> 22.3 us
    ppermute x15, waiting for transfers between devices: 15.2 us -> 6.6 us  [swap(): return lax.ppermute(value, axis, [(i, i ^ mask) for i in range(size)])]
    ppermute x15, starting transfers between devices: 20.6 us -> 22.3 us  [swap(): return lax.ppermute(value, axis, [(i, i ^ mask) for i in range(size)])]
    pallas_call x2 -> x1, Pallas kernels: 13.9 us -> 12.4 us  [final_core(): pl.pallas_call(functools.partial(final_kernel, sample, place), in_specs=[...]
    pallas_call x1, Pallas kernels: 8.59 us -> 7.8 us  [core_partial(): pl.pallas_call(functools.partial(core_kernel, space, sample, block, chunk...]
    pallas_call x7 -> x6, Pallas kernels: 1.7 us -> 1.72 us  [small_call(): pl.pallas_call(body, in_specs=[vmem] * count + [anywhere] * len(after), o...]
  transfers between devices with their start and end apart: 15 -> 15, of which waited for: 5 -> 4; matrix products, arithmetic and copies ran while one was open for 0% -> 0% of each run, Pallas kernels for 34% -> 37%
where the time goes in v1:
time: 61.5 us; the launch traced here: 61.3 us
  Pallas kernels  31.7 us (52%)
  starting transfers between devices  22.3 us (36%)
  waiting for transfers between devices  6.6 us (11%)
  between operations  0.75 us (1%)
    ppermute x15, starting transfers between devices, swap(): return lax.ppermute(value, axis, [(i, i ^ mask) for i in range(size)])  22.3 us
    pallas_call x1, Pallas kernels, final_core(): pl.pallas_call(functools.partial(final_kernel, sample, place), in_specs=[...  12.4 us
    pallas_call x1, Pallas kernels, sketch_partial(): pl.pallas_call(functools.partial(sketch_kernel, space, sample, block), in...  9.69 us
    pallas_call x1, Pallas kernels, core_partial(): pl.pallas_call(functools.partial(core_kernel, space, sample, block, chunk...  7.8 us
    ppermute x15, waiting for transfers between devices, swap(): return lax.ppermute(value, axis, [(i, i ^ mask) for i in range(size)])  6.6 us
    pallas_call x6, Pallas kernels, small_call(): pl.pallas_call(body, in_specs=[vmem] * count + [anywhere] * len(after), o...  1.72 us
  transfers between devices with their start and end apart: 15, of which 4 were waited for; matrix products, arithmetic and copies ran while one was open for 0% of the time, Pallas kernels for 37%

profile of v1, /device:TPU:0, one launch (start us, length us, event | category | flops | bytes accessed | tf_op | source)
XLA Modules:
  0.0 61.3 jit_solution(14190092388793835045)
XLA Ops:
  0.6 7.8 %core_partial.1 = (f32[3072,128]{1,0:T(8,128)S(1)}, f32[3072,128]{1,0:T(8,128)S(1)}) custom-call(bf16[48,1,128,1024]{3,2,1,0:T(8,128)(2,1)} %x_hbm.3, bf16[1024,128]{1,0:T(8,128)(2,1)} %two_hbm.1, bf16[1024,128]{1,0:T(8,128)(2,1)} %one_hbm.1), custom_call_target="tpu_custom_call" | custom-call | flops 1 | bytes 1 | tf_op jit(solution)/shard_map/core_partial/pallas_call | solution.py:108
  8.4 0.5 collective-permute-start
  9.0 3.0 %collective-permute-done.refs_1_ = f32[3072,128]{1,0:T(8,128)S(1)} collective-permute-done((f32[3072,128]{1,0:T(8,128)S(1)}, f32[3072,128]{1,0:T(8,128)S(1)}, u32[]{:S(2)}, u32[]{:S(2)}) %collective-permute-start) | collective-permute-done | bytes 1572896 | tf_op jit(solution)/shard_map/ppermute | solution.py:354
  12.0 0.0 copy-start
  12.0 0.0 copy-start.1
  12.0 0.0 copy-start.2
  12.0 0.0 copy-start.3
  12.0 0.2 add_core.3
  12.2 2.9 %collective-permute-start.1 = (f32[768,128]{1,0:T(8,128)S(1)}, f32[768,128]{1,0:T(8,128)S(1)}, u32[]{:S(2)}, u32[]{:S(2)}) collective-permute-start(f32[768,128]{1,0:T(8,128)S(1)} %get-tuple-element.41), channel_id=1, source_target_pairs={{0,8},{4,12},{8,0},{12,4},{16,24},{20,28},{24,16},{28,20},{1,9},{5... | collective-permute-start | bytes 1179656 | tf_op jit(solution)/shard_map/ppermute | solution.py:354
  15.1 1.5 %collective-permute-start.2 = (f32[768,128]{1,0:T(8,128)S(1)}, f32[768,128]{1,0:T(8,128)S(1)}, u32[]{:S(2)}, u32[]{:S(2)}) collective-permute-start(f32[768,128]{1,0:T(8,128)S(1)} %get-tuple-element.42), channel_id=1, source_target_pairs={{0,16},{4,20},{8,24},{12,28},{16,0},{20,4},{24,8},{28,12},{1,17},{... | collective-permute-start | bytes 1179656 | tf_op jit(solution)/shard_map/ppermute | solution.py:354
  16.6 0.0 copy-done
  16.6 0.0 copy-done.1
  16.6 0.0 copy-done.2
  16.6 0.0 copy-done.3
  16.6 9.7 %sketch_partial.1 = (f32[568,256]{1,0:T(8,128)S(1)}, f32[568,256]{1,0:T(8,128)S(1)}, f32[4,32,256]{2,1,0:T(8,128)S(1)}) custom-call(bf16[48,1,128,1024]{3,2,1,0:T(8,128)(2,1)} %x_hbm.3, bf16[128,256]{1,0:T(8,128)(2,1)S(1)} %copy-done.1, bf16[1024,256]{1,0:T(8,128)(2,1)S(1)} %copy-done, bf16[48,256]{1,0:T(8,128)(2,1)S(1)} %copy-done.2, ...), custom_call_target="tpu_custom_call" | custom-call | flops 1 | bytes 1 | tf_op jit(solution)/shard_map/sketch_partial/pallas_call | solution.py:219
  26.3 0.0 collective-permute-done.1.refs_1_
  26.3 0.0 collective-permute-done.2.refs_3_
  26.3 0.1 add_core.4
  26.5 0.1 collective-permute-start.3
  26.5 1.2 %collective-permute-start.10 = (f32[384,128]{1,0:T(8,128)S(1)}, f32[384,128]{1,0:T(8,128)S(1)}, u32[]{:S(2)}, u32[]{:S(2)}) collective-permute-start(f32[384,128]{1,0:T(8,128)S(1)} %get-tuple-element.60), channel_id=1, source_target_pairs={{0,16},{4,20},{8,24},{12,28},{16,0},{20,4},{24,8},{28,12},{1,17},{... | collective-permute-start | bytes 589832 | tf_op jit(solution)/shard_map/ppermute | solution.py:354
  27.7 0.5 collective-permute-start.11
  28.3 0.2 collective-permute-done.3.refs_1_
  28.5 0.1 add_cores.1
  28.6 1.3 %collective-permute-start.4 = (f32[184,256]{1,0:T(8,128)S(1)}, f32[184,256]{1,0:T(8,128)S(1)}, u32[]{:S(2)}, u32[]{:S(2)}) collective-permute-start(f32[184,256]{1,0:T(8,128)S(1)} %get-tuple-element.48), channel_id=1, source_target_pairs={{0,8},{4,12},{8,0},{12,4},{16,24},{20,28},{24,16},{28,20},{1,9},{5... | collective-permute-start | bytes 565256 | tf_op jit(solution)/shard_map/ppermute | solution.py:354
  29.9 0.9 %collective-permute-start.5 = (f32[184,256]{1,0:T(8,128)S(1)}, f32[184,256]{1,0:T(8,128)S(1)}, u32[]{:S(2)}, u32[]{:S(2)}) collective-permute-start(f32[184,256]{1,0:T(8,128)S(1)} %get-tuple-element.49), channel_id=1, source_target_pairs={{0,16},{4,20},{8,24},{12,28},{16,0},{20,4},{24,8},{28,12},{1,17},{... | collective-permute-start | bytes 565256 | tf_op jit(solution)/shard_map/ppermute | solution.py:354
  30.8 1.3 %collective-permute-start.6 = (f32[184,256]{1,0:T(8,128)S(1)}, f32[184,256]{1,0:T(8,128)S(1)}, u32[]{:S(2)}, u32[]{:S(2)}) collective-permute-start(f32[184,256]{1,0:T(8,128)S(1)} %get-tuple-element.50), channel_id=1, source_target_pairs={{0,24},{4,28},{8,16},{12,20},{16,8},{20,12},{24,0},{28,4},{1,25},{... | collective-permute-start | bytes 565256 | tf_op jit(solution)/shard_map/ppermute | solution.py:354
  32.2 2.1 %collective-permute-done.10.refs_1_ = f32[384,128]{1,0:T(8,128)S(1)} collective-permute-done((f32[384,128]{1,0:T(8,128)S(1)}, f32[384,128]{1,0:T(8,128)S(1)}, u32[]{:S(2)}, u32[]{:S(2)}) %collective-permute-start.10) | collective-permute-done | bytes 196640 | tf_op jit(solution)/shard_map/ppermute | solution.py:354
  34.3 1.2 %collective-permute-done.11.refs_3_ = f32[384,128]{1,0:T(8,128)S(1)} collective-permute-done((f32[384,128]{1,0:T(8,128)S(1)}, f32[384,128]{1,0:T(8,128)S(1)}, u32[]{:S(2)}, u32[]{:S(2)}) %collective-permute-start.11) | collective-permute-done | bytes 196640 | tf_op jit(solution)/shard_map/ppermute | solution.py:354
  35.5 1.7 %collective-permute-start.12 = (f32[192,128]{1,0:T(8,128)S(1)}, f32[192,128]{1,0:T(8,128)S(1)}, u32[]{:S(2)}, u32[]{:S(2)}) collective-permute-start(f32[192,128]{1,0:T(8,128)S(1)} %get-tuple-element.63), channel_id=1, source_target_pairs={{0,1},{1,0},{2,3},{3,2},{4,5},{5,4},{6,7},{7,6},{8,9},{9,8},{10,11... | collective-permute-start | bytes 294920 | tf_op jit(solution)/shard_map/ppermute | solution.py:354
  37.2 2.6 %collective-permute-start.13 = (f32[192,128]{1,0:T(8,128)S(1)}, f32[192,128]{1,0:T(8,128)S(1)}, u32[]{:S(2)}, u32[]{:S(2)}) collective-permute-start(f32[192,128]{1,0:T(8,128)S(1)} %get-tuple-element.64), channel_id=1, source_target_pairs={{0,2},{1,3},{2,0},{3,1},{4,6},{5,7},{6,4},{7,5},{8,10},{9,11},{10,... | collective-permute-start | bytes 294920 | tf_op jit(solution)/shard_map/ppermute | solution.py:354
  39.8 0.0 collective-permute-done.4.refs_1_
  39.8 3.4 %collective-permute-start.14 = (f32[192,128]{1,0:T(8,128)S(1)}, f32[192,128]{1,0:T(8,128)S(1)}, u32[]{:S(2)}, u32[]{:S(2)}) collective-permute-start(f32[192,128]{1,0:T(8,128)S(1)} %get-tuple-element.65), channel_id=1, source_target_pairs={{0,3},{1,2},{2,1},{3,0},{4,7},{5,6},{6,5},{7,4},{8,11},{9,10},{10,... | collective-permute-start | bytes 294920 | tf_op jit(solution)/shard_map/ppermute | solution.py:354
  43.1 0.0 collective-permute-done.5.refs_2_
  43.1 0.0 collective-permute-done.6.refs_3_
  43.1 0.6 %add_chips.1 = (f32[112,256]{1,0:T(8,128)S(1)}, f32[112,256]{1,0:T(8,128)S(1)}, f32[112,256]{1,0:T(8,128)S(1)}, f32[112,256]{1,0:T(8,128)S(1)}, f32[1,256]{1,0:T(1,128)}) custom-call(f32[184,256]{1,0:T(8,128)S(1)} %get-tuple-element.47.refs_0_.refs_4_, f32[184,256]{1,0:T(8,128)S(1)} %collective-permute-done.4.refs_1_, ...), custom_call_target="tpu_custom_call" | custom-call | flops 1 | bytes 1 | tf_op jit(solution)/shard_map/add_chips/pallas_call | solution.py:364
  43.8 1.6 %collective-permute-start.7 = (f32[112,256]{1,0:T(8,128)S(1)}, f32[112,256]{1,0:T(8,128)S(1)}, u32[]{:S(2)}, u32[]{:S(2)}) collective-permute-start(f32[112,256]{1,0:T(8,128)S(1)} %get-tuple-element.52), channel_id=1, source_target_pairs={{0,1},{1,0},{2,3},{3,2},{4,5},{5,4},{6,7},{7,6},{8,9},{9,8},{10,11... | collective-permute-start | bytes 344072 | tf_op jit(solution)/shard_map/ppermute | solution.py:354
  45.3 2.6 %collective-permute-start.8 = (f32[112,256]{1,0:T(8,128)S(1)}, f32[112,256]{1,0:T(8,128)S(1)}, u32[]{:S(2)}, u32[]{:S(2)}) collective-permute-start(f32[112,256]{1,0:T(8,128)S(1)} %get-tuple-element.53), channel_id=1, source_target_pairs={{0,2},{1,3},{2,0},{3,1},{4,6},{5,7},{6,4},{7,5},{8,10},{9,11},{10,... | collective-permute-start | bytes 344072 | tf_op jit(solution)/shard_map/ppermute | solution.py:354
  47.9 0.0 collective-permute-done.12.refs_1_
  47.9 0.2 collective-permute-start.9
  48.2 0.0 collective-permute-done.13.refs_2_
  48.2 0.0 collective-permute-done.14.refs_3_
  48.2 0.0 copy-done.4
  48.2 0.0 copy-done.5
  48.2 12.4 %final_core.1 = (f32[128,512,128]{2,1,0:T(8,128)}, f32[8,128]{1,0:T(8,128)}) custom-call(f32[192,128]{1,0:T(8,128)S(1)} %get-tuple-element.62.refs_0_, f32[192,128]{1,0:T(8,128)S(1)} %collective-permute-done.12.refs_1_, f32[192,128]{1,0:T(8,128)S(1)} %collective-permute-done.13.refs_2_, f32[192,128]{1,0:T(8,128)S(1)} %collective-permute-done.14.refs_3_, ...), custom_call_target="tpu_custom_call" | custom-call | flops 1073741824 | bytes 33554432 | tf_op jit(solution)/shard_map/final_core/pallas_call | solution.py:329
  60.6 0.0 collective-permute-done.7.refs_1_
  60.6 0.0 collective-permute-done.8.refs_2_
  60.6 0.0 collective-permute-done.9.refs_3_
  60.7 0.7 %add_samples.1 = (f32[64,128]{1,0:T(8,128)}, f32[32,256]{1,0:T(8,128)}, f32[48,256]{1,0:T(8,128)}) custom-call(f32[112,256]{1,0:T(8,128)S(1)} %get-tuple-element.51.refs_0_.refs_6_, f32[112,256]{1,0:T(8,128)S(1)} %collective-permute-done.7.refs_1_, f32[112,256]{1,0:T(8,128)S(1)} %collective-permute-done.8.refs_2_, f32[112,256]{1,0:T(8,128)S(1)} %collective-permute-done.9.refs_3_), custom_call_target="tpu_custom_call" | custom-call | flops 1 | bytes 1 | tf_op jit(solution)/shard_map/add_samples/pallas_call | solution.py:364
  (3 shorter events, 0.0 us)
Async XLA Ops:
  8.4 3.6 %collective-permute-start = (f32[3072,128]{1,0:T(8,128)S(1)}, f32[3072,128]{1,0:T(8,128)S(1)}, u32[]{:S(2)}, u32[]{:S(2)}) collective-permute-start(f32[3072,128]{1,0:T(8,128)S(1)} %get-tuple-element.37), channel_id=1, source_target_pairs={{0,4},{4,0},{8,12},{12,8},{16,20},{20,16},{24,28},{28,24},{1,5},{5... | collective-permute-start | bytes 4718600 | tf_op jit(solution)/shard_map/ppermute | solution.py:354
  12.0 4.6 %copy-start = (bf16[1024,256]{1,0:T(8,128)(2,1)S(1)}, bf16[1024,256]{1,0:T(8,128)(2,1)}, u32[]{:S(2)}) copy-start(bf16[1024,256]{1,0:T(8,128)(2,1)} %two_ref.1) | copy-start | bytes 1572868
  12.0 4.6 %copy-start.1 = (bf16[128,256]{1,0:T(8,128)(2,1)S(1)}, bf16[128,256]{1,0:T(8,128)(2,1)}, u32[]{:S(2)}) copy-start(bf16[128,256]{1,0:T(8,128)(2,1)} %one_ref.1) | copy-start | bytes 196612
  12.0 4.6 %copy-start.2 = (bf16[48,256]{1,0:T(8,128)(2,1)S(1)}, bf16[48,256]{1,0:T(8,128)(2,1)}, u32[]{:S(2)}) copy-start(bf16[48,256]{1,0:T(8,128)(2,1)} %three_ref.1) | copy-start | bytes 73732
  12.0 4.6 %copy-start.3 = (bf16[1,256]{1,0:T(2,128)(2,1)S(1)}, bf16[1,256]{1,0:T(2,128)(2,1)}, u32[]{:S(2)}) copy-start(bf16[1,256]{1,0:T(2,128)(2,1)} %four_ref.1) | copy-start | bytes 1540
  12.2 14.2 %collective-permute-start.1 = (f32[768,128]{1,0:T(8,128)S(1)}, f32[768,128]{1,0:T(8,128)S(1)}, u32[]{:S(2)}, u32[]{:S(2)}) collective-permute-start(f32[768,128]{1,0:T(8,128)S(1)} %get-tuple-element.41), channel_id=1, source_target_pairs={{0,8},{4,12},{8,0},{12,4},{16,24},{20,28},{24,16},{28,20},{1,9},{5... | collective-permute-start | bytes 1179656 | tf_op jit(solution)/shard_map/ppermute | solution.py:354
  15.1 11.2 %collective-permute-start.2 = (f32[768,128]{1,0:T(8,128)S(1)}, f32[768,128]{1,0:T(8,128)S(1)}, u32[]{:S(2)}, u32[]{:S(2)}) collective-permute-start(f32[768,128]{1,0:T(8,128)S(1)} %get-tuple-element.42), channel_id=1, source_target_pairs={{0,16},{4,20},{8,24},{12,28},{16,0},{20,4},{24,8},{28,12},{1,17},{... | collective-permute-start | bytes 1179656 | tf_op jit(solution)/shard_map/ppermute | solution.py:354
  26.5 2.1 %collective-permute-start.3 = (f32[568,256]{1,0:T(8,128)S(1)}, f32[568,256]{1,0:T(8,128)S(1)}, u32[]{:S(2)}, u32[]{:S(2)}) collective-permute-start(f32[568,256]{1,0:T(8,128)S(1)} %get-tuple-element.45), channel_id=1, source_target_pairs={{0,4},{4,0},{8,12},{12,8},{16,20},{20,16},{24,28},{28,24},{1,5},{5... | collective-permute-start | bytes 1744904 | tf_op jit(solution)/shard_map/ppermute | solution.py:354
  26.5 7.8 %collective-permute-start.10 = (f32[384,128]{1,0:T(8,128)S(1)}, f32[384,128]{1,0:T(8,128)S(1)}, u32[]{:S(2)}, u32[]{:S(2)}) collective-permute-start(f32[384,128]{1,0:T(8,128)S(1)} %get-tuple-element.60), channel_id=1, source_target_pairs={{0,16},{4,20},{8,24},{12,28},{16,0},{20,4},{24,8},{28,12},{1,17},{... | collective-permute-start | bytes 589832 | tf_op jit(solution)/shard_map/ppermute | solution.py:354
  27.7 7.7 %collective-permute-start.11 = (f32[384,128]{1,0:T(8,128)S(1)}, f32[384,128]{1,0:T(8,128)S(1)}, u32[]{:S(2)}, u32[]{:S(2)}) collective-permute-start(f32[384,128]{1,0:T(8,128)S(1)} %get-tuple-element.61), channel_id=1, source_target_pairs={{0,8},{4,12},{8,0},{12,4},{16,24},{20,28},{24,16},{28,20},{1,9},{5... | collective-permute-start | bytes 589832 | tf_op jit(solution)/shard_map/ppermute | solution.py:354
  28.5 19.6 %copy-start.4 = (bf16[48,128]{1,0:T(8,128)(2,1)S(1)}, bf16[48,128]{1,0:T(8,128)(2,1)}, u32[]{:S(2)}) copy-start(bf16[48,128]{1,0:T(8,128)(2,1)} %refs_4_.1) | copy-start | bytes 36868
  28.5 19.6 %copy-start.5 = (bf16[4,128]{1,0:T(4,128)(2,1)S(1)}, bf16[4,128]{1,0:T(4,128)(2,1)}, u32[]{:S(2)}) copy-start(bf16[4,128]{1,0:T(4,128)(2,1)} %refs_5_.1) | copy-start | bytes 3076
  28.6 11.1 %collective-permute-start.4 = (f32[184,256]{1,0:T(8,128)S(1)}, f32[184,256]{1,0:T(8,128)S(1)}, u32[]{:S(2)}, u32[]{:S(2)}) collective-permute-start(f32[184,256]{1,0:T(8,128)S(1)} %get-tuple-element.48), channel_id=1, source_target_pairs={{0,8},{4,12},{8,0},{12,4},{16,24},{20,28},{24,16},{28,20},{1,9},{5... | collective-permute-start | bytes 565256 | tf_op jit(solution)/shard_map/ppermute | solution.py:354
  29.9 13.2 %collective-permute-start.5 = (f32[184,256]{1,0:T(8,128)S(1)}, f32[184,256]{1,0:T(8,128)S(1)}, u32[]{:S(2)}, u32[]{:S(2)}) collective-permute-start(f32[184,256]{1,0:T(8,128)S(1)} %get-tuple-element.49), channel_id=1, source_target_pairs={{0,16},{4,20},{8,24},{12,28},{16,0},{20,4},{24,8},{28,12},{1,17},{... | collective-permute-start | bytes 565256 | tf_op jit(solution)/shard_map/ppermute | solution.py:354
  30.8 12.3 %collective-permute-start.6 = (f32[184,256]{1,0:T(8,128)S(1)}, f32[184,256]{1,0:T(8,128)S(1)}, u32[]{:S(2)}, u32[]{:S(2)}) collective-permute-start(f32[184,256]{1,0:T(8,128)S(1)} %get-tuple-element.50), channel_id=1, source_target_pairs={{0,24},{4,28},{8,16},{12,20},{16,8},{20,12},{24,0},{28,4},{1,25},{... | collective-permute-start | bytes 565256 | tf_op jit(solution)/shard_map/ppermute | solution.py:354
  35.5 12.4 %collective-permute-start.12 = (f32[192,128]{1,0:T(8,128)S(1)}, f32[192,128]{1,0:T(8,128)S(1)}, u32[]{:S(2)}, u32[]{:S(2)}) collective-permute-start(f32[192,128]{1,0:T(8,128)S(1)} %get-tuple-element.63), channel_id=1, source_target_pairs={{0,1},{1,0},{2,3},{3,2},{4,5},{5,4},{6,7},{7,6},{8,9},{9,8},{10,11... | collective-permute-start | bytes 294920 | tf_op jit(solution)/shard_map/ppermute | solution.py:354
  37.2 11.0 %collective-permute-start.13 = (f32[192,128]{1,0:T(8,128)S(1)}, f32[192,128]{1,0:T(8,128)S(1)}, u32[]{:S(2)}, u32[]{:S(2)}) collective-permute-start(f32[192,128]{1,0:T(8,128)S(1)} %get-tuple-element.64), channel_id=1, source_target_pairs={{0,2},{1,3},{2,0},{3,1},{4,6},{5,7},{6,4},{7,5},{8,10},{9,11},{10,... | collective-permute-start | bytes 294920 | tf_op jit(solution)/shard_map/ppermute | solution.py:354
  39.8 8.4 %collective-permute-start.14 = (f32[192,128]{1,0:T(8,128)S(1)}, f32[192,128]{1,0:T(8,128)S(1)}, u32[]{:S(2)}, u32[]{:S(2)}) collective-permute-start(f32[192,128]{1,0:T(8,128)S(1)} %get-tuple-element.65), channel_id=1, source_target_pairs={{0,3},{1,2},{2,1},{3,0},{4,7},{5,6},{6,5},{7,4},{8,11},{9,10},{10,... | collective-permute-start | bytes 294920 | tf_op jit(solution)/shard_map/ppermute | solution.py:354
  43.8 16.9 %collective-permute-start.7 = (f32[112,256]{1,0:T(8,128)S(1)}, f32[112,256]{1,0:T(8,128)S(1)}, u32[]{:S(2)}, u32[]{:S(2)}) collective-permute-start(f32[112,256]{1,0:T(8,128)S(1)} %get-tuple-element.52), channel_id=1, source_target_pairs={{0,1},{1,0},{2,3},{3,2},{4,5},{5,4},{6,7},{7,6},{8,9},{9,8},{10,11... | collective-permute-start | bytes 344072 | tf_op jit(solution)/shard_map/ppermute | solution.py:354
  45.3 15.3 %collective-permute-start.8 = (f32[112,256]{1,0:T(8,128)S(1)}, f32[112,256]{1,0:T(8,128)S(1)}, u32[]{:S(2)}, u32[]{:S(2)}) collective-permute-start(f32[112,256]{1,0:T(8,128)S(1)} %get-tuple-element.53), channel_id=1, source_target_pairs={{0,2},{1,3},{2,0},{3,1},{4,6},{5,7},{6,4},{7,5},{8,10},{9,11},{10,... | collective-permute-start | bytes 344072 | tf_op jit(solution)/shard_map/ppermute | solution.py:354
  47.9 12.7 %collective-permute-start.9 = (f32[112,256]{1,0:T(8,128)S(1)}, f32[112,256]{1,0:T(8,128)S(1)}, u32[]{:S(2)}, u32[]{:S(2)}) collective-permute-start(f32[112,256]{1,0:T(8,128)S(1)} %get-tuple-element.54), channel_id=1, source_target_pairs={{0,3},{1,2},{2,1},{3,0},{4,7},{5,6},{6,5},{7,4},{8,11},{9,10},{10,... | collective-permute-start | bytes 344072 | tf_op jit(solution)/shard_map/ppermute | solution.py:354

commit v2 on v1

--- a/solution.py
+++ b/solution.py
@@ -129,11 +129,12 @@
 
 
 def sketch_kernel(
-    space, sample, block, x_hbm, one_ref, two_ref, three_ref, four_ref, after_ref,
-    keep_ref, send_ref, first_ref,
+    space, sample, block, x_hbm, one_ref, two_ref, three_ref, four_ref, c_three_ref, c_four_ref, after_ref,
+    keep_ref, send_ref, first_ref, final_left_ref, final_base_ref,
     x_ref, acc_one, acc_two, acc_u, pairs, flipped, one_t, turned, sems,
 ):
     del after_ref
+    me, my = lax.axis_index("space"), lax.axis_index("sample")
     times, points, cols = x_ref.shape
     width = two_ref.shape[1]
     count = times // block
@@ -154,6 +155,7 @@
     if points < 128:
         one = jnp.concatenate([one, jnp.zeros((128 - points, width), F32)], axis=0)
     one_t[...] = one.T[:, :points]
+    final_constants(sample, my, c_three_ref, c_four_ref, final_left_ref, final_base_ref)
 
     start = 0
     for length in portions(times, block):
@@ -175,7 +177,6 @@
         acc_two[...] = acc_two[...] + more if start else more
         start += length
 
-    me, my = lax.axis_index("space"), lax.axis_index("sample")
     turned[...] = acc_two[...].T
     own = cols // (space * sample)
     for slot in range(space):
@@ -184,15 +185,8 @@
             place = (slot ^ me) * sample + (far ^ my)
             at = (slot // 2 * sample + far) * own
             ref[at : at + own, :] = turned[pl.ds(pl.multiple_of(place * own, own), own), :]
-    u = acc_u[...]
-    three = three_ref[...].astype(F32)
-    tail = space // 2 * sample * own
-    third = u * four_ref[...].astype(F32)
-    fourth = jnp.sum(u * three, axis=0, keepdims=True)
-    fourth = jnp.concatenate([fourth, jnp.zeros((7, width), F32)], axis=0)
     for ref in (keep_ref, send_ref):
-        ref[tail : tail + times, :] = third
-        ref[tail + times :, :] = fourth
+        ref[space // 2 * sample * own :, :] = acc_u[...]
     narrow, folds = width // sample, width // points
     lines = narrow // folds
     square = acc_one[...]
@@ -208,21 +202,27 @@
 
 
 def sketch_partial(
-    ensemble, map_one, map_two, map_three, map_four, after, space, sample, block
+    ensemble, map_one, map_two, map_three, map_four, core_three, core_four, after, space, sample, block
 ):
     times, _, points, cols = ensemble.shape
-    width = map_two.shape[1]
+    width, rank = map_two.shape[1], core_three.shape[1]
     own = cols // (space * sample)
-    shape = jax.ShapeDtypeStruct((space // 2 * sample * own + times + 8, width), F32)
+    shape = jax.ShapeDtypeStruct((space // 2 * sample * own + times, width), F32)
     first = jax.ShapeDtypeStruct((sample, points // sample, width), F32)
     anywhere = pl.BlockSpec(memory_space=pl.ANY)
     return pl.pallas_call(
         functools.partial(sketch_kernel, space, sample, block),
         in_specs=[pl.BlockSpec(memory_space=pltpu.HBM)]
-        + [pl.BlockSpec(memory_space=pltpu.VMEM)] * 4
+        + [pl.BlockSpec(memory_space=pltpu.VMEM)] * 6
         + [anywhere],
-        out_specs=[pl.BlockSpec(memory_space=pltpu.VMEM)] * 3,
-        out_shape=[shape, shape, first],
+        out_specs=[pl.BlockSpec(memory_space=pltpu.VMEM)] * 5,
+        out_shape=[
+            shape,
+            shape,
+            first,
+            jax.ShapeDtypeStruct((rank, 2 * times), BF16),
+            jax.ShapeDtypeStruct((2 * rank, 2 * rank), F32),
+        ],
         scratch_shapes=[
             pltpu.VMEM((times, points, cols), BF16),
             pltpu.VMEM((points, width), F32),
@@ -239,25 +239,17 @@
         name="sketch_partial",
     )(
         pltpu.with_memory_space_constraint(ensemble, pltpu.HBM),
-        map_one, map_two, map_three, map_four, after,
-    )
-
-
-def final_kernel(sample, place, *refs):
-    start, first, count, _ = place
-    *ins, out_hbm, token_ref, left_ref, base_ref, ring, sems = refs
-    parts, (three_ref, four_ref) = ins[:sample], ins[sample : sample + 2]
+        map_one, map_two, map_three, map_four, core_three, core_four, after,
+    )
+
+
+def final_constants(sample, my, three_ref, four_ref, left_ref, base_ref):
     times, rank = three_ref.shape
     wide = rank // sample
-    slots, each = ring.shape[0], ring.shape[1]
-    span = each // (2 * sample)
-    my = lax.axis_index("sample")
-
-    token_ref[...] = jnp.zeros_like(token_ref)
     three = three_ref[...].astype(F32)
     three = jnp.concatenate([three, jnp.zeros((rank - times, rank), F32)], axis=0).T
     three = three[:, :times].astype(BF16)
-    three = jnp.concatenate([three, three], axis=1)
+    left_ref[...] = jnp.concatenate([three, three], axis=1)
     four = four_ref[...].astype(F32)
     which = lax.broadcasted_iota(jnp.int32, (sample, rank), 0)
     odd = lax.broadcasted_iota(jnp.int32, (wide, 2 * rank), 0) % 2
@@ -268,14 +260,25 @@
         line = jnp.concatenate([line, line], axis=1)
         pieces.append(jnp.where(odd == side, line, 0.0))
     base_ref[...] = jnp.concatenate(pieces * 2, axis=0)
+
+
+def final_kernel(sample, place, *refs):
+    start, first, count, _ = place
+    *ins, out_hbm, left_ref, ring, sems = refs
+    parts, (three_ref, base_ref) = ins[:sample][::-1], ins[sample : sample + 2]
+    rank, times = three_ref.shape[0], three_ref.shape[1] // 2
+    wide = rank // sample
+    slots, each = ring.shape[0], ring.shape[1]
+    step = 2 * sample
+    span = each // step
     row = (lax.broadcasted_iota(jnp.int32, base_ref.shape, 0) % wide) // 2
 
-    def copy(b, slot, group):
+    def copy(b, slot, m, group):
         at = pl.multiple_of((first + b) * rank, rank)
         return pltpu.make_async_copy(
-            ring.at[slot],
-            out_hbm.at[pl.ds(group * each, each), pl.ds(at, rank)],
-            sems.at[slot],
+            ring.at[slot, pl.ds(m * step, step)],
+            out_hbm.at[pl.ds(group * each + m * step, step), pl.ds(at, rank)],
+            sems.at[slot * span + m],
         )
 
     groups = rank // each
@@ -289,7 +292,7 @@
             joined += [h[:, g * wide : (g + 1) * wide] for h in held]
         high, low = split(jnp.concatenate(joined, axis=1))
         both = jnp.concatenate([high, low], axis=0)
-        high, low = split(jnp.dot(three, both, preferred_element_type=F32))
+        high, low = split(jnp.dot(three_ref[...], both, preferred_element_type=F32))
         for g in range(sample):
             at = slice(g * rank, (g + 1) * rank)
             left_ref[at, :] = jnp.concatenate([high[:, at], low[:, at]], axis=1)
@@ -300,28 +303,30 @@
 
                 @pl.when((b > 0) | (n > 0))
                 def _():
-                    copy(0, slot, 0).wait()
+                    for m in range(span):
+                        copy(0, slot, m, 0).wait()
 
                 for m in range(span):
                     right = jnp.where(row == group * span + m, base_ref[...], 0.0).astype(BF16)
                     out = jnp.dot(left_ref[...], right, preferred_element_type=F32)
                     for g in range(sample):
                         for k in range(2):
-                            ring[slot, m * 2 * sample + 2 * g + k] = out[
+                            ring[slot, m * step + 2 * g + k] = out[
                                 g * rank : (g + 1) * rank, k * rank : (k + 1) * rank
                             ]
-                copy(b, slot, group).start()
+                    copy(b, slot, m, group).start()
 
         lax.fori_loop(0, groups // slots, some, None)
 
     pl.loop(0, count)(block)
     for slot in range(slots):
-        copy(0, slot, 0).wait()
-
-
-def final_core(parts, core_three, core_four, after, place, into):
+        for m in range(span):
+            copy(0, slot, m, 0).wait()
+
+
+def final_core(parts, three, base, after, place, into):
     sample = len(parts)
-    rank = core_three.shape[1]
+    rank = three.shape[0]
     vmem, anywhere = pl.BlockSpec(memory_space=pltpu.VMEM), pl.BlockSpec(memory_space=pl.ANY)
     extra = list(after) + ([into] if into is not None else [])
     each = min(rank, 2 * sample * SPAN)
@@ -329,16 +334,12 @@
     return pl.pallas_call(
         functools.partial(final_kernel, sample, place),
         in_specs=[vmem] * (sample + 2) + [anywhere] * len(extra),
-        out_specs=[anywhere, vmem],
-        out_shape=[
-            jax.ShapeDtypeStruct((rank, place[3] * rank, rank), F32),
-            jax.ShapeDtypeStruct((8, 128), F32),
-        ],
+        out_specs=anywhere,
+        out_shape=jax.ShapeDtypeStruct((rank, place[3] * rank, rank), F32),
         scratch_shapes=[
             pltpu.VMEM((sample * rank, 2 * rank), BF16),
-            pltpu.VMEM((2 * rank, 2 * rank), F32),
             pltpu.VMEM((slots, each, rank, rank), F32),
-            pltpu.SemaphoreType.DMA((slots,)),
+            pltpu.SemaphoreType.DMA((slots * each // (2 * sample),)),
         ],
         input_output_aliases={sample + 1 + len(extra): 0} if into is not None else {},
         compiler_params=pltpu.CompilerParams(vmem_limit_bytes=32 * MIB),
@@ -346,7 +347,7 @@
             flops=4 * rank**4, bytes_accessed=4 * place[2] * rank**3, transcendentals=0
         ),
         name="final_core",
-    )(*parts, core_three, core_four, *extra)
+    )(*parts[::-1], three, base, *extra)
 
 
 def swap(value, axis, mask):
@@ -450,22 +451,25 @@
         out[rows:, :] = end
 
 
-def mix_kernel(sample, own, times, count, *refs):
-    ins, first_ref, outs, fourth_ref = refs[:count], refs[count], refs[count + 1 : -1], refs[-1]
+def mix_kernel(sample, own, count, *refs):
+    ins, (first_ref, three_ref, four_ref), outs = refs[:count][::-1], refs[count : count + 3], refs[count + 3 :]
+    *outs, fourth_ref = outs
     total = ins[0][...]
     for ref in ins[1:]:
         total = total + ref[...]
-    tail = sample * own
-    third = total[tail : tail + times]
+    times = three_ref.shape[0]
+    u = total[sample * own :]
+    third = u * four_ref[...].astype(F32)
     for far in range(sample):
         outs[far][:own, :] = total[far * own : (far + 1) * own]
         outs[far][own : own + times, :] = third
         outs[far][own + times :, :] = first_ref[far]
-    fourth_ref[...] = total[tail + times : tail + times + 1]
+    fourth_ref[...] = jnp.sum(u * three_ref[...].astype(F32), axis=0, keepdims=True)
 
 
 def end_kernel(sample, own, times, *refs):
-    ins, (one_ref, two_ref, three_ref) = refs[:sample], refs[sample:]
+    ins, (mid_ref, one_ref, two_ref, three_ref, four_ref) = refs[:sample], refs[sample:]
+    four_ref[...] = mid_ref[...]
     total = ins[0][...]
     for ref in ins[1:]:
         total = total + ref[...]
@@ -513,18 +517,18 @@
             else:
                 state[k] = [swap(p, "sample", far) if far else p for far, p in enumerate(outs)]
         if n == 0:
-            mine, send, first = sketch_partial(
-                ensemble, map_one, map_two, map_three, map_four, last, space, sample, BLOCK
+            mine, send, first, turned, base = sketch_partial(
+                ensemble, map_one, map_two, map_three, map_four, core_three, core_four, last,
+                space, sample, BLOCK,
             )
             last = first
         if n == min(1, len(stages) - 1):
             theirs = swap(send, "space", 1)
-            tail = times + 8
-            lines = (mine.shape[0] - tail) // chips
+            lines = (mine.shape[0] - times) // chips
             own = lines // sample
             pieces = small_call(
-                functools.partial(add_kernel, list(range(chips)), lines, tail),
-                [(lines + tail, width)] * chips, "add_cores", [mine, theirs], [last],
+                functools.partial(add_kernel, list(range(chips)), lines, times),
+                [(lines + times, width)] * chips, "add_cores", [mine, theirs], [last],
             )
             last = pieces[0]
             pieces = [swap(p, "space", 2 * u) if u else p for u, p in enumerate(pieces)]
@@ -533,18 +537,18 @@
     piece = total // chunks
     length = own + times + first.shape[1]
     *pieces, fourth = small_call(
-        functools.partial(mix_kernel, sample, own, times, chips),
-        [(length, width)] * sample + [(1, width)], "add_chips", [*pieces, first],
+        functools.partial(mix_kernel, sample, own, chips),
+        [(length, width)] * sample + [(1, width)], "add_chips",
+        [*pieces[::-1], first, map_three, map_four],
     )
     core = None
     for k in every:
-        core, _ = final_core(
-            state[k], core_three, core_four, [pieces[0]], (0, k * piece, piece, total), core
-        )
+        core = final_core(state[k], turned, base, [pieces[0]], (0, k * piece, piece, total), core)
     pieces = [swap(p, "sample", far) if far else p for far, p in enumerate(pieces)]
-    one, two, three = small_call(
+    one, two, three, fourth = small_call(
         functools.partial(end_kernel, sample, own, times),
-        [(width // sample, points), (own, width), (times, width)], "add_samples", pieces,
+        [(width // sample, points), (own, width), (times, width), (1, width)], "add_samples",
+        [*pieces, fourth],
     )
     return (one.T, two, three, fourth, core)
 

time: 61.5 us -> 59.5 us (0.967)
  starting transfers between devices: 22.3 us -> 19.9 us
  waiting for transfers between devices: 6.6 us -> 8.28 us
  Pallas kernels: 31.7 us -> 30.4 us
    ppermute x15, starting transfers between devices: 22.3 us -> 19.9 us  [swap(): return lax.ppermute(value, axis, [(i, i ^ mask) for i in range(size)])]
    ppermute x15, waiting for transfers between devices: 6.6 us -> 8.28 us  [swap(): return lax.ppermute(value, axis, [(i, i ^ mask) for i in range(size)])]
    pallas_call x1, Pallas kernels: 12.4 us -> 11.6 us  [final_core(): pl.pallas_call(functools.partial(final_kernel, sample, place), in_specs=[...]
  transfers between devices with their start and end apart: 15 -> 15, of which waited for: 4 -> 7; matrix products, arithmetic and copies ran while one was open for 0% -> 0% of each run, Pallas kernels for 37% -> 36%
where the time goes in v2:
time: 59.5 us; the launch traced here: 59.3 us
  Pallas kernels  30.4 us (51%)
  starting transfers between devices  19.9 us (33%)
  waiting for transfers between devices  8.28 us (14%)
  between operations  0.77 us (1%)
    ppermute x15, starting transfers between devices, swap(): return lax.ppermute(value, axis, [(i, i ^ mask) for i in range(size)])  19.9 us
    pallas_call x1, Pallas kernels, final_core(): pl.pallas_call(functools.partial(final_kernel, sample, place), in_specs=[...  11.6 us
    pallas_call x1, Pallas kernels, sketch_partial(): pl.pallas_call(functools.partial(sketch_kernel, space, sample, block), in...  9.82 us
    ppermute x15, waiting for transfers between devices, swap(): return lax.ppermute(value, axis, [(i, i ^ mask) for i in range(size)])  8.28 us
    pallas_call x1, Pallas kernels, core_partial(): pl.pallas_call(functools.partial(core_kernel, space, sample, block, chunk...  7.8 us
  transfers between devices with their start and end apart: 15, of which 7 were waited for; matrix products, arithmetic and copies ran while one was open for 0% of the time, Pallas kernels for 36%

profile of v2, /device:TPU:0, one launch (start us, length us, event | category | flops | bytes accessed | tf_op | source)
XLA Modules:
  0.0 59.3 jit_solution(16670894448200995997)
XLA Ops:
  0.6 7.8 %core_partial.1 = (f32[3072,128]{1,0:T(8,128)S(1)}, f32[3072,128]{1,0:T(8,128)S(1)}) custom-call(bf16[48,1,128,1024]{3,2,1,0:T(8,128)(2,1)} %x_hbm.3, bf16[1024,128]{1,0:T(8,128)(2,1)} %two_hbm.1, bf16[1024,128]{1,0:T(8,128)(2,1)} %one_hbm.1), custom_call_target="tpu_custom_call" | custom-call | flops 1 | bytes 1 | tf_op jit(solution)/shard_map/core_partial/pallas_call | solution.py:108
  8.4 0.5 collective-permute-start
  9.0 3.0 %collective-permute-done.refs_1_ = f32[3072,128]{1,0:T(8,128)S(1)} collective-permute-done((f32[3072,128]{1,0:T(8,128)S(1)}, f32[3072,128]{1,0:T(8,128)S(1)}, u32[]{:S(2)}, u32[]{:S(2)}) %collective-permute-start) | collective-permute-done | bytes 1572896 | tf_op jit(solution)/shard_map/ppermute | solution.py:355
  12.0 0.0 copy-start
  12.0 0.0 copy-start.1
  12.0 0.0 copy-start.2
  12.0 0.0 copy-start.5
  12.0 0.2 add_core.3
  12.2 2.9 %collective-permute-start.1 = (f32[768,128]{1,0:T(8,128)S(1)}, f32[768,128]{1,0:T(8,128)S(1)}, u32[]{:S(2)}, u32[]{:S(2)}) collective-permute-start(f32[768,128]{1,0:T(8,128)S(1)} %get-tuple-element.43), channel_id=1, source_target_pairs={{0,8},{4,12},{8,0},{12,4},{16,24},{20,28},{24,16},{28,20},{1,9},{5... | collective-permute-start | bytes 1179656 | tf_op jit(solution)/shard_map/ppermute | solution.py:355
  15.1 1.5 %collective-permute-start.2 = (f32[768,128]{1,0:T(8,128)S(1)}, f32[768,128]{1,0:T(8,128)S(1)}, u32[]{:S(2)}, u32[]{:S(2)}) collective-permute-start(f32[768,128]{1,0:T(8,128)S(1)} %get-tuple-element.44), channel_id=1, source_target_pairs={{0,16},{4,20},{8,24},{12,28},{16,0},{20,4},{24,8},{28,12},{1,17},{... | collective-permute-start | bytes 1179656 | tf_op jit(solution)/shard_map/ppermute | solution.py:355
  16.6 0.0 copy-done
  16.6 0.0 copy-done.1
  16.6 0.0 copy-done.2
  16.6 0.0 copy-done.3
  16.6 0.0 copy-done.4
  16.7 0.0 copy-done.5
  16.7 9.8 %sketch_partial.1 = (f32[560,256]{1,0:T(8,128)S(1)}, f32[560,256]{1,0:T(8,128)S(1)}, f32[4,32,256]{2,1,0:T(8,128)S(1)}, bf16[128,96]{1,0:T(8,128)(2,1)S(1)}, f32[256,256]{1,0:T(8,128)S(1)}) custom-call(bf16[48,1,128,1024]{3,2,1,0:T(8,128)(2,1)} %x_hbm.3, bf16[128,256]{1,0:T(8,128)(2,1)S(1)} %copy-done.2, bf16[1024,256]{1,0:T(8,128)(2,1)S(1)} %copy-done, ...), custom_call_target="tpu_custom_call" | custom-call | flops 1 | bytes 1 | tf_op jit(solution)/shard_map/sketch_partial/pallas_call | solution.py:213
  26.5 0.0 collective-permute-done.1.refs_1_
  26.5 0.0 collective-permute-done.2.refs_3_
  26.5 0.1 add_core.4
  26.6 0.1 collective-permute-start.3
  26.7 1.0 %collective-permute-start.10 = (f32[384,128]{1,0:T(8,128)S(1)}, f32[384,128]{1,0:T(8,128)S(1)}, u32[]{:S(2)}, u32[]{:S(2)}) collective-permute-start(f32[384,128]{1,0:T(8,128)S(1)} %get-tuple-element.63), channel_id=1, source_target_pairs={{0,16},{4,20},{8,24},{12,28},{16,0},{20,4},{24,8},{28,12},{1,17},{... | collective-permute-start | bytes 589832 | tf_op jit(solution)/shard_map/ppermute | solution.py:355
  27.8 0.5 collective-permute-start.11
  28.3 0.4 collective-permute-done.3.refs_1_
  28.7 0.1 add_cores.1
  28.8 1.7 %collective-permute-start.4 = (f32[176,256]{1,0:T(8,128)S(1)}, f32[176,256]{1,0:T(8,128)S(1)}, u32[]{:S(2)}, u32[]{:S(2)}) collective-permute-start(f32[176,256]{1,0:T(8,128)S(1)} %get-tuple-element.49), channel_id=1, source_target_pairs={{0,24},{4,28},{8,16},{12,20},{16,8},{20,12},{24,0},{28,4},{1,25},{... | collective-permute-start | bytes 540680 | tf_op jit(solution)/shard_map/ppermute | solution.py:355
  30.4 1.0 %collective-permute-start.5 = (f32[176,256]{1,0:T(8,128)S(1)}, f32[176,256]{1,0:T(8,128)S(1)}, u32[]{:S(2)}, u32[]{:S(2)}) collective-permute-start(f32[176,256]{1,0:T(8,128)S(1)} %get-tuple-element.50), channel_id=1, source_target_pairs={{0,16},{4,20},{8,24},{12,28},{16,0},{20,4},{24,8},{28,12},{1,17},{... | collective-permute-start | bytes 540680 | tf_op jit(solution)/shard_map/ppermute | solution.py:355
  31.4 0.9 %collective-permute-start.6 = (f32[176,256]{1,0:T(8,128)S(1)}, f32[176,256]{1,0:T(8,128)S(1)}, u32[]{:S(2)}, u32[]{:S(2)}) collective-permute-start(f32[176,256]{1,0:T(8,128)S(1)} %get-tuple-element.51), channel_id=1, source_target_pairs={{0,8},{4,12},{8,0},{12,4},{16,24},{20,28},{24,16},{28,20},{1,9},{5... | collective-permute-start | bytes 540680 | tf_op jit(solution)/shard_map/ppermute | solution.py:355
  32.3 2.2 %collective-permute-done.10.refs_1_ = f32[384,128]{1,0:T(8,128)S(1)} collective-permute-done((f32[384,128]{1,0:T(8,128)S(1)}, f32[384,128]{1,0:T(8,128)S(1)}, u32[]{:S(2)}, u32[]{:S(2)}) %collective-permute-start.10) | collective-permute-done | bytes 196640 | tf_op jit(solution)/shard_map/ppermute | solution.py:355
  34.5 1.0 %collective-permute-done.11.refs_3_ = f32[384,128]{1,0:T(8,128)S(1)} collective-permute-done((f32[384,128]{1,0:T(8,128)S(1)}, f32[384,128]{1,0:T(8,128)S(1)}, u32[]{:S(2)}, u32[]{:S(2)}) %collective-permute-start.11) | collective-permute-done | bytes 196640 | tf_op jit(solution)/shard_map/ppermute | solution.py:355
  35.6 3.7 %collective-permute-start.12 = (f32[192,128]{1,0:T(8,128)S(1)}, f32[192,128]{1,0:T(8,128)S(1)}, u32[]{:S(2)}, u32[]{:S(2)}) collective-permute-start(f32[192,128]{1,0:T(8,128)S(1)} %get-tuple-element.65), channel_id=1, source_target_pairs={{0,3},{1,2},{2,1},{3,0},{4,7},{5,6},{6,5},{7,4},{8,11},{9,10},{10,... | collective-permute-start | bytes 294920 | tf_op jit(solution)/shard_map/ppermute | solution.py:355
  39.2 0.0 collective-permute-start.13
  39.2 0.7 %collective-permute-done.4.refs_0_ = f32[176,256]{1,0:T(8,128)S(1)} collective-permute-done((f32[176,256]{1,0:T(8,128)S(1)}, f32[176,256]{1,0:T(8,128)S(1)}, u32[]{:S(2)}, u32[]{:S(2)}) %collective-permute-start.4) | collective-permute-done | bytes 180256 | tf_op jit(solution)/shard_map/ppermute | solution.py:355
  39.9 1.6 %collective-permute-start.14 = (f32[192,128]{1,0:T(8,128)S(1)}, f32[192,128]{1,0:T(8,128)S(1)}, u32[]{:S(2)}, u32[]{:S(2)}) collective-permute-start(f32[192,128]{1,0:T(8,128)S(1)} %get-tuple-element.67), channel_id=1, source_target_pairs={{0,1},{1,0},{2,3},{3,2},{4,5},{5,4},{6,7},{7,6},{8,9},{9,8},{10,11... | collective-permute-start | bytes 294920 | tf_op jit(solution)/shard_map/ppermute | solution.py:355
  41.5 0.3 collective-permute-done.5.refs_1_
  41.8 0.7 %collective-permute-done.6.refs_2_ = f32[176,256]{1,0:T(8,128)S(1)} collective-permute-done((f32[176,256]{1,0:T(8,128)S(1)}, f32[176,256]{1,0:T(8,128)S(1)}, u32[]{:S(2)}, u32[]{:S(2)}) %collective-permute-start.6) | collective-permute-done | bytes 180256 | tf_op jit(solution)/shard_map/ppermute | solution.py:355
  42.5 0.1 add_chips.1
  42.6 1.7 %collective-permute-start.7 = (f32[112,256]{1,0:T(8,128)S(1)}, f32[112,256]{1,0:T(8,128)S(1)}, u32[]{:S(2)}, u32[]{:S(2)}) collective-permute-start(f32[112,256]{1,0:T(8,128)S(1)} %get-tuple-element.54), channel_id=1, source_target_pairs={{0,1},{1,0},{2,3},{3,2},{4,5},{5,4},{6,7},{7,6},{8,9},{9,8},{10,11... | collective-permute-start | bytes 344072 | tf_op jit(solution)/shard_map/ppermute | solution.py:355
  44.2 2.6 %collective-permute-start.8 = (f32[112,256]{1,0:T(8,128)S(1)}, f32[112,256]{1,0:T(8,128)S(1)}, u32[]{:S(2)}, u32[]{:S(2)}) collective-permute-start(f32[112,256]{1,0:T(8,128)S(1)} %get-tuple-element.55), channel_id=1, source_target_pairs={{0,2},{1,3},{2,0},{3,1},{4,6},{5,7},{6,4},{7,5},{8,10},{9,11},{10,... | collective-permute-start | bytes 344072 | tf_op jit(solution)/shard_map/ppermute | solution.py:355
  46.8 0.0 collective-permute-done.12.refs_0_
  46.8 0.2 collective-permute-start.9
  47.0 0.0 collective-permute-done.13.refs_1_
  47.0 0.0 collective-permute-done.14.refs_2_
  47.0 11.6 %final_core.1 = f32[128,512,128]{2,1,0:T(8,128)} custom-call(f32[192,128]{1,0:T(8,128)S(1)} %collective-permute-done.12.refs_0_, f32[192,128]{1,0:T(8,128)S(1)} %collective-permute-done.13.refs_1_, f32[192,128]{1,0:T(8,128)S(1)} %collective-permute-done.14.refs_2_, f32[192,128]{1,0:T(8,128)S(1)} %get-tuple-element.68.refs_3_, ...), custom_call_target="tpu_custom_call" | custom-call | flops 1073741824 | bytes 33554432 | tf_op jit(solution)/shard_map/final_core/pallas_call | solution.py:334
  58.6 0.0 collective-permute-done.7.refs_1_
  58.7 0.0 collective-permute-done.8.refs_2_
  58.7 0.0 collective-permute-done.9.refs_3_
  58.7 0.7 %add_samples.1 = (f32[64,128]{1,0:T(8,128)}, f32[32,256]{1,0:T(8,128)}, f32[48,256]{1,0:T(8,128)}, f32[1,256]{1,0:T(1,128)}) custom-call(f32[112,256]{1,0:T(8,128)S(1)} %get-tuple-element.53.refs_0_.refs_6_, f32[112,256]{1,0:T(8,128)S(1)} %collective-permute-done.7.refs_1_, f32[112,256]{1,0:T(8,128)S(1)} %collective-permute-done.8.refs_2_, ...), custom_call_target="tpu_custom_call" | custom-call | flops 1 | bytes 1 | tf_op jit(solution)/shard_map/add_samples/pallas_call | solution.py:365
  (3 shorter events, 0.0 us)
Async XLA Ops:
  8.4 3.6 %collective-permute-start = (f32[3072,128]{1,0:T(8,128)S(1)}, f32[3072,128]{1,0:T(8,128)S(1)}, u32[]{:S(2)}, u32[]{:S(2)}) collective-permute-start(f32[3072,128]{1,0:T(8,128)S(1)} %get-tuple-element.39), channel_id=1, source_target_pairs={{0,4},{4,0},{8,12},{12,8},{16,20},{20,16},{24,28},{28,24},{1,5},{5... | collective-permute-start | bytes 4718600 | tf_op jit(solution)/shard_map/ppermute | solution.py:355
  12.0 4.6 %copy-start = (bf16[1024,256]{1,0:T(8,128)(2,1)S(1)}, bf16[1024,256]{1,0:T(8,128)(2,1)}, u32[]{:S(2)}) copy-start(bf16[1024,256]{1,0:T(8,128)(2,1)} %two_ref.1) | copy-start | bytes 1572868
  12.0 4.6 %copy-start.1 = (bf16[48,256]{1,0:T(8,128)(2,1)S(1)}, bf16[48,256]{1,0:T(8,128)(2,1)}, u32[]{:S(2)}) copy-start(bf16[48,256]{1,0:T(8,128)(2,1)} %refs_5_.1) | copy-start | bytes 73732
  12.0 4.6 %copy-start.2 = (bf16[128,256]{1,0:T(8,128)(2,1)S(1)}, bf16[128,256]{1,0:T(8,128)(2,1)}, u32[]{:S(2)}) copy-start(bf16[128,256]{1,0:T(8,128)(2,1)} %one_ref.1) | copy-start | bytes 196612
  12.0 4.6 %copy-start.3 = (bf16[48,128]{1,0:T(8,128)(2,1)S(1)}, bf16[48,128]{1,0:T(8,128)(2,1)}, u32[]{:S(2)}) copy-start(bf16[48,128]{1,0:T(8,128)(2,1)} %c_three_ref.1) | copy-start | bytes 36868
  12.0 4.6 %copy-start.4 = (bf16[1,256]{1,0:T(2,128)(2,1)S(1)}, bf16[1,256]{1,0:T(2,128)(2,1)}, u32[]{:S(2)}) copy-start(bf16[1,256]{1,0:T(2,128)(2,1)} %refs_6_.1) | copy-start | bytes 1540
  12.0 4.6 %copy-start.5 = (bf16[4,128]{1,0:T(4,128)(2,1)S(1)}, bf16[4,128]{1,0:T(4,128)(2,1)}, u32[]{:S(2)}) copy-start(bf16[4,128]{1,0:T(4,128)(2,1)} %c_four_ref.1) | copy-start | bytes 3076
  12.2 14.3 %collective-permute-start.1 = (f32[768,128]{1,0:T(8,128)S(1)}, f32[768,128]{1,0:T(8,128)S(1)}, u32[]{:S(2)}, u32[]{:S(2)}) collective-permute-start(f32[768,128]{1,0:T(8,128)S(1)} %get-tuple-element.43), channel_id=1, source_target_pairs={{0,8},{4,12},{8,0},{12,4},{16,24},{20,28},{24,16},{28,20},{1,9},{5... | collective-permute-start | bytes 1179656 | tf_op jit(solution)/shard_map/ppermute | solution.py:355
  15.1 11.4 %collective-permute-start.2 = (f32[768,128]{1,0:T(8,128)S(1)}, f32[768,128]{1,0:T(8,128)S(1)}, u32[]{:S(2)}, u32[]{:S(2)}) collective-permute-start(f32[768,128]{1,0:T(8,128)S(1)} %get-tuple-element.44), channel_id=1, source_target_pairs={{0,16},{4,20},{8,24},{12,28},{16,0},{20,4},{24,8},{28,12},{1,17},{... | collective-permute-start | bytes 1179656 | tf_op jit(solution)/shard_map/ppermute | solution.py:355
  26.6 2.0 %collective-permute-start.3 = (f32[560,256]{1,0:T(8,128)S(1)}, f32[560,256]{1,0:T(8,128)S(1)}, u32[]{:S(2)}, u32[]{:S(2)}) collective-permute-start(f32[560,256]{1,0:T(8,128)S(1)} %get-tuple-element.47), channel_id=1, source_target_pairs={{0,4},{4,0},{8,12},{12,8},{16,20},{20,16},{24,28},{28,24},{1,5},{5... | collective-permute-start | bytes 1720328 | tf_op jit(solution)/shard_map/ppermute | solution.py:355
  26.7 7.8 %collective-permute-start.10 = (f32[384,128]{1,0:T(8,128)S(1)}, f32[384,128]{1,0:T(8,128)S(1)}, u32[]{:S(2)}, u32[]{:S(2)}) collective-permute-start(f32[384,128]{1,0:T(8,128)S(1)} %get-tuple-element.63), channel_id=1, source_target_pairs={{0,16},{4,20},{8,24},{12,28},{16,0},{20,4},{24,8},{28,12},{1,17},{... | collective-permute-start | bytes 589832 | tf_op jit(solution)/shard_map/ppermute | solution.py:355
  27.8 7.7 %collective-permute-start.11 = (f32[384,128]{1,0:T(8,128)S(1)}, f32[384,128]{1,0:T(8,128)S(1)}, u32[]{:S(2)}, u32[]{:S(2)}) collective-permute-start(f32[384,128]{1,0:T(8,128)S(1)} %get-tuple-element.64), channel_id=1, source_target_pairs={{0,8},{4,12},{8,0},{12,4},{16,24},{20,28},{24,16},{28,20},{1,9},{5... | collective-permute-start | bytes 589832 | tf_op jit(solution)/shard_map/ppermute | solution.py:355
  28.8 11.1 %collective-permute-start.4 = (f32[176,256]{1,0:T(8,128)S(1)}, f32[176,256]{1,0:T(8,128)S(1)}, u32[]{:S(2)}, u32[]{:S(2)}) collective-permute-start(f32[176,256]{1,0:T(8,128)S(1)} %get-tuple-element.49), channel_id=1, source_target_pairs={{0,24},{4,28},{8,16},{12,20},{16,8},{20,12},{24,0},{28,4},{1,25},{... | collective-permute-start | bytes 540680 | tf_op jit(solution)/shard_map/ppermute | solution.py:355
  30.4 11.3 %collective-permute-start.5 = (f32[176,256]{1,0:T(8,128)S(1)}, f32[176,256]{1,0:T(8,128)S(1)}, u32[]{:S(2)}, u32[]{:S(2)}) collective-permute-start(f32[176,256]{1,0:T(8,128)S(1)} %get-tuple-element.50), channel_id=1, source_target_pairs={{0,16},{4,20},{8,24},{12,28},{16,0},{20,4},{24,8},{28,12},{1,17},{... | collective-permute-start | bytes 540680 | tf_op jit(solution)/shard_map/ppermute | solution.py:355
  31.4 11.1 %collective-permute-start.6 = (f32[176,256]{1,0:T(8,128)S(1)}, f32[176,256]{1,0:T(8,128)S(1)}, u32[]{:S(2)}, u32[]{:S(2)}) collective-permute-start(f32[176,256]{1,0:T(8,128)S(1)} %get-tuple-element.51), channel_id=1, source_target_pairs={{0,8},{4,12},{8,0},{12,4},{16,24},{20,28},{24,16},{28,20},{1,9},{5... | collective-permute-start | bytes 540680 | tf_op jit(solution)/shard_map/ppermute | solution.py:355
  35.6 11.3 %collective-permute-start.12 = (f32[192,128]{1,0:T(8,128)S(1)}, f32[192,128]{1,0:T(8,128)S(1)}, u32[]{:S(2)}, u32[]{:S(2)}) collective-permute-start(f32[192,128]{1,0:T(8,128)S(1)} %get-tuple-element.65), channel_id=1, source_target_pairs={{0,3},{1,2},{2,1},{3,0},{4,7},{5,6},{6,5},{7,4},{8,11},{9,10},{10,... | collective-permute-start | bytes 294920 | tf_op jit(solution)/shard_map/ppermute | solution.py:355
  39.2 7.8 %collective-permute-start.13 = (f32[192,128]{1,0:T(8,128)S(1)}, f32[192,128]{1,0:T(8,128)S(1)}, u32[]{:S(2)}, u32[]{:S(2)}) collective-permute-start(f32[192,128]{1,0:T(8,128)S(1)} %get-tuple-element.66), channel_id=1, source_target_pairs={{0,2},{1,3},{2,0},{3,1},{4,6},{5,7},{6,4},{7,5},{8,10},{9,11},{10,... | collective-permute-start | bytes 294920 | tf_op jit(solution)/shard_map/ppermute | solution.py:355
  39.9 7.1 %collective-permute-start.14 = (f32[192,128]{1,0:T(8,128)S(1)}, f32[192,128]{1,0:T(8,128)S(1)}, u32[]{:S(2)}, u32[]{:S(2)}) collective-permute-start(f32[192,128]{1,0:T(8,128)S(1)} %get-tuple-element.67), channel_id=1, source_target_pairs={{0,1},{1,0},{2,3},{3,2},{4,5},{5,4},{6,7},{7,6},{8,9},{9,8},{10,11... | collective-permute-start | bytes 294920 | tf_op jit(solution)/shard_map/ppermute | solution.py:355
  42.6 16.1 %collective-permute-start.7 = (f32[112,256]{1,0:T(8,128)S(1)}, f32[112,256]{1,0:T(8,128)S(1)}, u32[]{:S(2)}, u32[]{:S(2)}) collective-permute-start(f32[112,256]{1,0:T(8,128)S(1)} %get-tuple-element.54), channel_id=1, source_target_pairs={{0,1},{1,0},{2,3},{3,2},{4,5},{5,4},{6,7},{7,6},{8,9},{9,8},{10,11... | collective-permute-start | bytes 344072 | tf_op jit(solution)/shard_map/ppermute | solution.py:355
  44.2 14.4 %collective-permute-start.8 = (f32[112,256]{1,0:T(8,128)S(1)}, f32[112,256]{1,0:T(8,128)S(1)}, u32[]{:S(2)}, u32[]{:S(2)}) collective-permute-start(f32[112,256]{1,0:T(8,128)S(1)} %get-tuple-element.55), channel_id=1, source_target_pairs={{0,2},{1,3},{2,0},{3,1},{4,6},{5,7},{6,4},{7,5},{8,10},{9,11},{10,... | collective-permute-start | bytes 344072 | tf_op jit(solution)/shard_map/ppermute | solution.py:355
  46.8 11.9 %collective-permute-start.9 = (f32[112,256]{1,0:T(8,128)S(1)}, f32[112,256]{1,0:T(8,128)S(1)}, u32[]{:S(2)}, u32[]{:S(2)}) collective-permute-start(f32[112,256]{1,0:T(8,128)S(1)} %get-tuple-element.56), channel_id=1, source_target_pairs={{0,3},{1,2},{2,1},{3,0},{4,7},{5,6},{6,5},{7,4},{8,11},{9,10},{10,... | collective-permute-start | bytes 344072 | tf_op jit(solution)/shard_map/ppermute | solution.py:355

commit v3 on v2

--- a/solution.py
+++ b/solution.py
@@ -108,10 +108,9 @@
     return pl.pallas_call(
         functools.partial(core_kernel, space, sample, block, chunks),
         in_specs=[hbm] * 3,
-        out_specs=[pl.BlockSpec(memory_space=pltpu.VMEM)] * (2 * chunks),
-        out_shape=[shape] * (2 * chunks),
+        out_specs=[pl.BlockSpec(memory_space=pltpu.VMEM)] * (2 * chunks + 1),
+        out_shape=[shape] * (2 * chunks) + [pltpu.VMEM((times, points, width), BF16)],
         scratch_shapes=[
-            pltpu.VMEM((times, points, width), BF16),
             pltpu.VMEM(core_two.shape, BF16),
             pltpu.VMEM((points, rank), BF16),
             pltpu.VMEM((rank, width), BF16),
@@ -129,23 +128,14 @@
 
 
 def sketch_kernel(
-    space, sample, block, x_hbm, one_ref, two_ref, three_ref, four_ref, c_three_ref, c_four_ref, after_ref,
+    space, sample, block, x_ref, one_ref, two_ref, three_ref, four_ref, c_three_ref, c_four_ref, after_ref,
     keep_ref, send_ref, first_ref, final_left_ref, final_base_ref,
-    x_ref, acc_one, acc_two, acc_u, pairs, flipped, one_t, turned, sems,
+    acc_one, acc_two, acc_u, pairs, flipped, one_t, turned,
 ):
     del after_ref
     me, my = lax.axis_index("space"), lax.axis_index("sample")
     times, points, cols = x_ref.shape
     width = two_ref.shape[1]
-    count = times // block
-    loads = [
-        pltpu.make_async_copy(
-            x_hbm.at[pl.ds(n * block, block), 0], x_ref.at[pl.ds(n * block, block)], sems.at[n]
-        )
-        for n in range(count)
-    ]
-    for load in loads:
-        load.start()
     four = four_ref[...].astype(F32)
     pair = three_ref[...].astype(F32) * four
     pairs[...] = pair
@@ -159,8 +149,6 @@
 
     start = 0
     for length in portions(times, block):
-        for n in range(start // block, (start + length) // block):
-            loads[n].wait()
         x = x_ref[start : start + length].reshape(length * points, cols)
         proj = jnp.dot(x, two_ref[...], preferred_element_type=F32)
         one = one_ref[...].astype(F32)
@@ -202,9 +190,9 @@
 
 
 def sketch_partial(
-    ensemble, map_one, map_two, map_three, map_four, core_three, core_four, after, space, sample, block
+    held, map_one, map_two, map_three, map_four, core_three, core_four, after, space, sample, block
 ):
-    times, _, points, cols = ensemble.shape
+    times, points, cols = held.shape
     width, rank = map_two.shape[1], core_three.shape[1]
     own = cols // (space * sample)
     shape = jax.ShapeDtypeStruct((space // 2 * sample * own + times, width), F32)
@@ -212,19 +200,16 @@
     anywhere = pl.BlockSpec(memory_space=pl.ANY)
     return pl.pallas_call(
         functools.partial(sketch_kernel, space, sample, block),
-        in_specs=[pl.BlockSpec(memory_space=pltpu.HBM)]
-        + [pl.BlockSpec(memory_space=pltpu.VMEM)] * 6
-        + [anywhere],
+        in_specs=[pl.BlockSpec(memory_space=pltpu.VMEM)] * 7 + [anywhere],
         out_specs=[pl.BlockSpec(memory_space=pltpu.VMEM)] * 5,
         out_shape=[
-            shape,
-            shape,
-            first,
-            jax.ShapeDtypeStruct((rank, 2 * times), BF16),
-            jax.ShapeDtypeStruct((2 * rank, 2 * rank), F32),
+            pltpu.VMEM(shape.shape, F32),
+            pltpu.VMEM(shape.shape, F32),
+            pltpu.VMEM(first.shape, F32),
+            pltpu.VMEM((rank, 2 * times), BF16),
+            pltpu.VMEM((2 * rank, 2 * rank), F32),
         ],
         scratch_shapes=[
-            pltpu.VMEM((times, points, cols), BF16),
             pltpu.VMEM((points, width), F32),
             pltpu.VMEM((width, cols), F32),
             pltpu.VMEM((times, width), F32),
@@ -232,13 +217,12 @@
             pltpu.VMEM((width, 128), F32),
             pltpu.VMEM((width, points), F32),
             pltpu.VMEM((cols, width), F32),
-            pltpu.SemaphoreType.DMA((times // block,)),
         ],
         compiler_params=pltpu.CompilerParams(vmem_limit_bytes=32 * MIB),
         cost_estimate=LIGHT,
         name="sketch_partial",
     )(
-        pltpu.with_memory_space_constraint(ensemble, pltpu.HBM),
+        pltpu.with_memory_space_constraint(held, pltpu.VMEM),
         map_one, map_two, map_three, map_four, core_three, core_four, after,
     )
 
@@ -493,7 +477,7 @@
     chunks = min(CHUNKS, rank // (space * sample))
     every = range(chunks)
 
-    sent = core_partial(ensemble, core_one, core_two, space, sample, BLOCK, chunks)
+    *sent, held = core_partial(ensemble, core_one, core_two, space, sample, BLOCK, chunks)
     keep, send = sent[:chunks], sent[chunks:]
     got = [swap(s, "space", 1) for s in send]
     stages = core_tree(space, sample)
@@ -518,7 +502,7 @@
                 state[k] = [swap(p, "sample", far) if far else p for far, p in enumerate(outs)]
         if n == 0:
             mine, send, first, turned, base = sketch_partial(
-                ensemble, map_one, map_two, map_three, map_four, core_three, core_four, last,
+                held, map_one, map_two, map_three, map_four, core_three, core_four, last,
                 space, sample, BLOCK,
             )
             last = first

time: 59.5 us -> 59.8 us (level)
  Pallas kernels: 30.4 us -> 27.9 us
  waiting for transfers between devices: 8.28 us -> 10.4 us
    pallas_call x1, Pallas kernels: 9.82 us -> 7.19 us  [sketch_partial(): pl.pallas_call(functools.partial(sketch_kernel, space, sample, block), in...]
    ppermute x15, waiting for transfers between devices: 8.28 us -> 10.4 us  [swap(): return lax.ppermute(value, axis, [(i, i ^ mask) for i in range(size)])]
  transfers between devices with their start and end apart: 15 -> 15, of which waited for: 7 -> 8; matrix products, arithmetic and copies ran while one was open for 0% -> 0% of each run, Pallas kernels for 36% -> 32%
where the time goes in v3:
time: 59.8 us; the launch traced here: 59.6 us
  Pallas kernels  27.9 us (47%)
  starting transfers between devices  20.4 us (34%)
  waiting for transfers between devices  10.4 us (17%)
  between operations  0.79 us (1%)
    ppermute x15, starting transfers between devices, swap(): return lax.ppermute(value, axis, [(i, i ^ mask) for i in range(size)])  20.4 us
    pallas_call x1, Pallas kernels, final_core(): pl.pallas_call(functools.partial(final_kernel, sample, place), in_specs=[...  11.6 us
    ppermute x15, waiting for transfers between devices, swap(): return lax.ppermute(value, axis, [(i, i ^ mask) for i in range(size)])  10.4 us
    pallas_call x1, Pallas kernels, core_partial(): pl.pallas_call(functools.partial(core_kernel, space, sample, block, chunk...  7.84 us
    pallas_call x1, Pallas kernels, sketch_partial(): pl.pallas_call(functools.partial(sketch_kernel, space, sample, block), in...  7.19 us
    pallas_call x6, Pallas kernels, small_call(): pl.pallas_call(body, in_specs=[vmem] * count + [anywhere] * len(after), o...  1.32 us
  transfers between devices with their start and end apart: 15, of which 8 were waited for; matrix products, arithmetic and copies ran while one was open for 0% of the time, Pallas kernels for 32%

profile of v3, /device:TPU:0, one launch (start us, length us, event | category | flops | bytes accessed | tf_op | source)
XLA Modules:
  0.0 59.6 jit_solution(10383362772080616372)
XLA Ops:
  0.6 0.0 copy-start.4
  0.6 0.0 copy-start.1
  0.7 0.0 copy-start.5
  0.7 0.0 copy-start.3
  0.7 0.0 copy-start
  0.7 0.0 copy-start.2
  0.7 7.8 %core_partial.1 = (f32[3072,128]{1,0:T(8,128)S(1)}, f32[3072,128]{1,0:T(8,128)S(1)}, bf16[48,128,1024]{2,1,0:T(8,128)(2,1)S(1)}) custom-call(bf16[48,1,128,1024]{3,2,1,0:T(8,128)(2,1)} %x_hbm.1, bf16[1024,128]{1,0:T(8,128)(2,1)} %two_hbm.1, bf16[1024,128]{1,0:T(8,128)(2,1)} %one_hbm.1), custom_call_target="tpu_custom_call" | custom-call | flops 1 | bytes 1 | tf_op jit(solution)/shard_map/core_partial/pallas_call | solution.py:108
  8.5 0.5 collective-permute-start
  9.1 3.0 %collective-permute-done.refs_1_ = f32[3072,128]{1,0:T(8,128)S(1)} collective-permute-done((f32[3072,128]{1,0:T(8,128)S(1)}, f32[3072,128]{1,0:T(8,128)S(1)}, u32[]{:S(2)}, u32[]{:S(2)}) %collective-permute-start) | collective-permute-done | bytes 1572896 | tf_op jit(solution)/shard_map/ppermute | solution.py:339
  12.1 0.2 add_core.3
  12.3 2.9 %collective-permute-start.1 = (f32[768,128]{1,0:T(8,128)S(1)}, f32[768,128]{1,0:T(8,128)S(1)}, u32[]{:S(2)}, u32[]{:S(2)}) collective-permute-start(f32[768,128]{1,0:T(8,128)S(1)} %get-tuple-element.45), channel_id=1, source_target_pairs={{0,8},{4,12},{8,0},{12,4},{16,24},{20,28},{24,16},{28,20},{1,9},{5... | collective-permute-start | bytes 1179656 | tf_op jit(solution)/shard_map/ppermute | solution.py:339
  15.2 1.5 %collective-permute-start.2 = (f32[768,128]{1,0:T(8,128)S(1)}, f32[768,128]{1,0:T(8,128)S(1)}, u32[]{:S(2)}, u32[]{:S(2)}) collective-permute-start(f32[768,128]{1,0:T(8,128)S(1)} %get-tuple-element.46), channel_id=1, source_target_pairs={{0,16},{4,20},{8,24},{12,28},{16,0},{20,4},{24,8},{28,12},{1,17},{... | collective-permute-start | bytes 1179656 | tf_op jit(solution)/shard_map/ppermute | solution.py:339
  16.7 0.0 copy-done.4
  16.7 0.0 copy-done.1
  16.7 0.0 copy-done
  16.7 0.0 copy-done.2
  16.7 7.2 %sketch_partial.1 = (f32[560,256]{1,0:T(8,128)S(1)}, f32[560,256]{1,0:T(8,128)S(1)}, f32[4,32,256]{2,1,0:T(8,128)S(1)}, bf16[128,96]{1,0:T(8,128)(2,1)S(1)}, f32[256,256]{1,0:T(8,128)S(1)}) custom-call(bf16[48,128,1024]{2,1,0:T(8,128)(2,1)S(1)} %get-tuple-element.39.x_ref, bf16[128,256]{1,0:T(8,128)(2,1)S(1)} %copy-done.2, bf16[1024,256]{1,0:T(8,128)(2,1)S(1)} %copy-done, ...), custom_call_target="tpu_custom_call" | custom-call | flops 1 | bytes 1 | tf_op jit(solution)/shard_map/sketch_partial/pallas_call | solution.py:201
  23.9 0.7 %collective-permute-done.1.refs_1_ = f32[768,128]{1,0:T(8,128)S(1)} collective-permute-done((f32[768,128]{1,0:T(8,128)S(1)}, f32[768,128]{1,0:T(8,128)S(1)}, u32[]{:S(2)}, u32[]{:S(2)}) %collective-permute-start.1) | collective-permute-done | bytes 393248 | tf_op jit(solution)/shard_map/ppermute | solution.py:339
  24.6 1.5 %collective-permute-done.2.refs_3_ = f32[768,128]{1,0:T(8,128)S(1)} collective-permute-done((f32[768,128]{1,0:T(8,128)S(1)}, f32[768,128]{1,0:T(8,128)S(1)}, u32[]{:S(2)}, u32[]{:S(2)}) %collective-permute-start.2) | collective-permute-done | bytes 393248 | tf_op jit(solution)/shard_map/ppermute | solution.py:339
  26.1 0.3 add_core.4
  26.4 0.1 collective-permute-start.3
  26.4 1.6 %collective-permute-start.10 = (f32[384,128]{1,0:T(8,128)S(1)}, f32[384,128]{1,0:T(8,128)S(1)}, u32[]{:S(2)}, u32[]{:S(2)}) collective-permute-start(f32[384,128]{1,0:T(8,128)S(1)} %get-tuple-element.65), channel_id=1, source_target_pairs={{0,16},{4,20},{8,24},{12,28},{16,0},{20,4},{24,8},{28,12},{1,17},{... | collective-permute-start | bytes 589832 | tf_op jit(solution)/shard_map/ppermute | solution.py:339
  28.0 0.5 collective-permute-start.11
  28.6 0.0 collective-permute-done.3.refs_1_
  28.6 0.1 add_cores.1
  28.7 1.5 %collective-permute-start.4 = (f32[176,256]{1,0:T(8,128)S(1)}, f32[176,256]{1,0:T(8,128)S(1)}, u32[]{:S(2)}, u32[]{:S(2)}) collective-permute-start(f32[176,256]{1,0:T(8,128)S(1)} %get-tuple-element.51), channel_id=1, source_target_pairs={{0,24},{4,28},{8,16},{12,20},{16,8},{20,12},{24,0},{28,4},{1,25},{... | collective-permute-start | bytes 540680 | tf_op jit(solution)/shard_map/ppermute | solution.py:339
  30.2 1.5 %collective-permute-start.5 = (f32[176,256]{1,0:T(8,128)S(1)}, f32[176,256]{1,0:T(8,128)S(1)}, u32[]{:S(2)}, u32[]{:S(2)}) collective-permute-start(f32[176,256]{1,0:T(8,128)S(1)} %get-tuple-element.52), channel_id=1, source_target_pairs={{0,16},{4,20},{8,24},{12,28},{16,0},{20,4},{24,8},{28,12},{1,17},{... | collective-permute-start | bytes 540680 | tf_op jit(solution)/shard_map/ppermute | solution.py:339
  31.7 0.5 collective-permute-start.6
  32.2 2.0 %collective-permute-done.10.refs_1_ = f32[384,128]{1,0:T(8,128)S(1)} collective-permute-done((f32[384,128]{1,0:T(8,128)S(1)}, f32[384,128]{1,0:T(8,128)S(1)}, u32[]{:S(2)}, u32[]{:S(2)}) %collective-permute-start.10) | collective-permute-done | bytes 196640 | tf_op jit(solution)/shard_map/ppermute | solution.py:339
  34.2 1.5 %collective-permute-done.11.refs_3_ = f32[384,128]{1,0:T(8,128)S(1)} collective-permute-done((f32[384,128]{1,0:T(8,128)S(1)}, f32[384,128]{1,0:T(8,128)S(1)}, u32[]{:S(2)}, u32[]{:S(2)}) %collective-permute-start.11) | collective-permute-done | bytes 196640 | tf_op jit(solution)/shard_map/ppermute | solution.py:339
  35.8 3.7 %collective-permute-start.12 = (f32[192,128]{1,0:T(8,128)S(1)}, f32[192,128]{1,0:T(8,128)S(1)}, u32[]{:S(2)}, u32[]{:S(2)}) collective-permute-start(f32[192,128]{1,0:T(8,128)S(1)} %get-tuple-element.67), channel_id=1, source_target_pairs={{0,3},{1,2},{2,1},{3,0},{4,7},{5,6},{6,5},{7,4},{8,11},{9,10},{10,... | collective-permute-start | bytes 294920 | tf_op jit(solution)/shard_map/ppermute | solution.py:339
  39.5 0.0 collective-permute-start.13
  39.5 0.1 collective-permute-done.4.refs_0_
  39.6 1.6 %collective-permute-start.14 = (f32[192,128]{1,0:T(8,128)S(1)}, f32[192,128]{1,0:T(8,128)S(1)}, u32[]{:S(2)}, u32[]{:S(2)}) collective-permute-start(f32[192,128]{1,0:T(8,128)S(1)} %get-tuple-element.69), channel_id=1, source_target_pairs={{0,1},{1,0},{2,3},{3,2},{4,5},{5,4},{6,7},{7,6},{8,9},{9,8},{10,11... | collective-permute-start | bytes 294920 | tf_op jit(solution)/shard_map/ppermute | solution.py:339
  41.2 0.3 collective-permute-done.5.refs_1_
  41.5 1.3 %collective-permute-done.6.refs_2_ = f32[176,256]{1,0:T(8,128)S(1)} collective-permute-done((f32[176,256]{1,0:T(8,128)S(1)}, f32[176,256]{1,0:T(8,128)S(1)}, u32[]{:S(2)}, u32[]{:S(2)}) %collective-permute-start.6) | collective-permute-done | bytes 180256 | tf_op jit(solution)/shard_map/ppermute | solution.py:339
  42.8 0.1 add_chips.1
  42.8 1.6 %collective-permute-start.7 = (f32[112,256]{1,0:T(8,128)S(1)}, f32[112,256]{1,0:T(8,128)S(1)}, u32[]{:S(2)}, u32[]{:S(2)}) collective-permute-start(f32[112,256]{1,0:T(8,128)S(1)} %get-tuple-element.56), channel_id=1, source_target_pairs={{0,1},{1,0},{2,3},{3,2},{4,5},{5,4},{6,7},{7,6},{8,9},{9,8},{10,11... | collective-permute-start | bytes 344072 | tf_op jit(solution)/shard_map/ppermute | solution.py:339
  44.5 2.6 %collective-permute-start.8 = (f32[112,256]{1,0:T(8,128)S(1)}, f32[112,256]{1,0:T(8,128)S(1)}, u32[]{:S(2)}, u32[]{:S(2)}) collective-permute-start(f32[112,256]{1,0:T(8,128)S(1)} %get-tuple-element.57), channel_id=1, source_target_pairs={{0,2},{1,3},{2,0},{3,1},{4,6},{5,7},{6,4},{7,5},{8,10},{9,11},{10,... | collective-permute-start | bytes 344072 | tf_op jit(solution)/shard_map/ppermute | solution.py:339
  47.1 0.0 collective-permute-done.12.refs_0_
  47.1 0.2 collective-permute-start.9
  47.3 0.0 collective-permute-done.13.refs_1_
  47.3 0.0 collective-permute-done.14.refs_2_
  47.3 11.6 %final_core.1 = f32[128,512,128]{2,1,0:T(8,128)} custom-call(f32[192,128]{1,0:T(8,128)S(1)} %collective-permute-done.12.refs_0_, f32[192,128]{1,0:T(8,128)S(1)} %collective-permute-done.13.refs_1_, f32[192,128]{1,0:T(8,128)S(1)} %collective-permute-done.14.refs_2_, f32[192,128]{1,0:T(8,128)S(1)} %get-tuple-element.70.refs_3_, ...), custom_call_target="tpu_custom_call" | custom-call | flops 1073741824 | bytes 33554432 | tf_op jit(solution)/shard_map/final_core/pallas_call | solution.py:318
  58.9 0.0 collective-permute-done.7.refs_1_
  58.9 0.0 collective-permute-done.8.refs_2_
  58.9 0.0 collective-permute-done.9.refs_3_
  58.9 0.7 %add_samples.1 = (f32[64,128]{1,0:T(8,128)}, f32[32,256]{1,0:T(8,128)}, f32[48,256]{1,0:T(8,128)}, f32[1,256]{1,0:T(1,128)}) custom-call(f32[112,256]{1,0:T(8,128)S(1)} %get-tuple-element.55.refs_0_.refs_6_, f32[112,256]{1,0:T(8,128)S(1)} %collective-permute-done.7.refs_1_, f32[112,256]{1,0:T(8,128)S(1)} %collective-permute-done.8.refs_2_, ...), custom_call_target="tpu_custom_call" | custom-call | flops 1 | bytes 1 | tf_op jit(solution)/shard_map/add_samples/pallas_call | solution.py:349
  (3 shorter events, 0.0 us)
Async XLA Ops:
  0.6 16.1 %copy-start.4 = (bf16[1,256]{1,0:T(2,128)(2,1)S(1)}, bf16[1,256]{1,0:T(2,128)(2,1)}, u32[]{:S(2)}) copy-start(bf16[1,256]{1,0:T(2,128)(2,1)} %refs_6_.1) | copy-start | bytes 1540
  0.6 16.1 %copy-start.1 = (bf16[48,256]{1,0:T(8,128)(2,1)S(1)}, bf16[48,256]{1,0:T(8,128)(2,1)}, u32[]{:S(2)}) copy-start(bf16[48,256]{1,0:T(8,128)(2,1)} %refs_5_.1) | copy-start | bytes 73732
  0.7 16.1 %copy-start.5 = (bf16[4,128]{1,0:T(4,128)(2,1)S(1)}, bf16[4,128]{1,0:T(4,128)(2,1)}, u32[]{:S(2)}) copy-start(bf16[4,128]{1,0:T(4,128)(2,1)} %c_four_ref.1) | copy-start | bytes 3076
  0.7 16.0 %copy-start.3 = (bf16[48,128]{1,0:T(8,128)(2,1)S(1)}, bf16[48,128]{1,0:T(8,128)(2,1)}, u32[]{:S(2)}) copy-start(bf16[48,128]{1,0:T(8,128)(2,1)} %c_three_ref.1) | copy-start | bytes 36868
  0.7 16.0 %copy-start = (bf16[1024,256]{1,0:T(8,128)(2,1)S(1)}, bf16[1024,256]{1,0:T(8,128)(2,1)}, u32[]{:S(2)}) copy-start(bf16[1024,256]{1,0:T(8,128)(2,1)} %two_ref.1) | copy-start | bytes 1572868
  0.7 16.0 %copy-start.2 = (bf16[128,256]{1,0:T(8,128)(2,1)S(1)}, bf16[128,256]{1,0:T(8,128)(2,1)}, u32[]{:S(2)}) copy-start(bf16[128,256]{1,0:T(8,128)(2,1)} %one_ref.1) | copy-start | bytes 196612
  8.5 3.6 %collective-permute-start = (f32[3072,128]{1,0:T(8,128)S(1)}, f32[3072,128]{1,0:T(8,128)S(1)}, u32[]{:S(2)}, u32[]{:S(2)}) collective-permute-start(f32[3072,128]{1,0:T(8,128)S(1)} %get-tuple-element.41), channel_id=1, source_target_pairs={{0,4},{4,0},{8,12},{12,8},{16,20},{20,16},{24,28},{28,24},{1,5},{5... | collective-permute-start | bytes 4718600 | tf_op jit(solution)/shard_map/ppermute | solution.py:339
  12.3 12.3 %collective-permute-start.1 = (f32[768,128]{1,0:T(8,128)S(1)}, f32[768,128]{1,0:T(8,128)S(1)}, u32[]{:S(2)}, u32[]{:S(2)}) collective-permute-start(f32[768,128]{1,0:T(8,128)S(1)} %get-tuple-element.45), channel_id=1, source_target_pairs={{0,8},{4,12},{8,0},{12,4},{16,24},{20,28},{24,16},{28,20},{1,9},{5... | collective-permute-start | bytes 1179656 | tf_op jit(solution)/shard_map/ppermute | solution.py:339
  15.2 10.9 %collective-permute-start.2 = (f32[768,128]{1,0:T(8,128)S(1)}, f32[768,128]{1,0:T(8,128)S(1)}, u32[]{:S(2)}, u32[]{:S(2)}) collective-permute-start(f32[768,128]{1,0:T(8,128)S(1)} %get-tuple-element.46), channel_id=1, source_target_pairs={{0,16},{4,20},{8,24},{12,28},{16,0},{20,4},{24,8},{28,12},{1,17},{... | collective-permute-start | bytes 1179656 | tf_op jit(solution)/shard_map/ppermute | solution.py:339
  26.4 2.2 %collective-permute-start.3 = (f32[560,256]{1,0:T(8,128)S(1)}, f32[560,256]{1,0:T(8,128)S(1)}, u32[]{:S(2)}, u32[]{:S(2)}) collective-permute-start(f32[560,256]{1,0:T(8,128)S(1)} %get-tuple-element.49), channel_id=1, source_target_pairs={{0,4},{4,0},{8,12},{12,8},{16,20},{20,16},{24,28},{28,24},{1,5},{5... | collective-permute-start | bytes 1720328 | tf_op jit(solution)/shard_map/ppermute | solution.py:339
  26.4 7.8 %collective-permute-start.10 = (f32[384,128]{1,0:T(8,128)S(1)}, f32[384,128]{1,0:T(8,128)S(1)}, u32[]{:S(2)}, u32[]{:S(2)}) collective-permute-start(f32[384,128]{1,0:T(8,128)S(1)} %get-tuple-element.65), channel_id=1, source_target_pairs={{0,16},{4,20},{8,24},{12,28},{16,0},{20,4},{24,8},{28,12},{1,17},{... | collective-permute-start | bytes 589832 | tf_op jit(solution)/shard_map/ppermute | solution.py:339
  28.0 7.7 %collective-permute-start.11 = (f32[384,128]{1,0:T(8,128)S(1)}, f32[384,128]{1,0:T(8,128)S(1)}, u32[]{:S(2)}, u32[]{:S(2)}) collective-permute-start(f32[384,128]{1,0:T(8,128)S(1)} %get-tuple-element.66), channel_id=1, source_target_pairs={{0,8},{4,12},{8,0},{12,4},{16,24},{20,28},{24,16},{28,20},{1,9},{5... | collective-permute-start | bytes 589832 | tf_op jit(solution)/shard_map/ppermute | solution.py:339
  28.7 11.0 %collective-permute-start.4 = (f32[176,256]{1,0:T(8,128)S(1)}, f32[176,256]{1,0:T(8,128)S(1)}, u32[]{:S(2)}, u32[]{:S(2)}) collective-permute-start(f32[176,256]{1,0:T(8,128)S(1)} %get-tuple-element.51), channel_id=1, source_target_pairs={{0,24},{4,28},{8,16},{12,20},{16,8},{20,12},{24,0},{28,4},{1,25},{... | collective-permute-start | bytes 540680 | tf_op jit(solution)/shard_map/ppermute | solution.py:339
  30.2 11.3 %collective-permute-start.5 = (f32[176,256]{1,0:T(8,128)S(1)}, f32[176,256]{1,0:T(8,128)S(1)}, u32[]{:S(2)}, u32[]{:S(2)}) collective-permute-start(f32[176,256]{1,0:T(8,128)S(1)} %get-tuple-element.52), channel_id=1, source_target_pairs={{0,16},{4,20},{8,24},{12,28},{16,0},{20,4},{24,8},{28,12},{1,17},{... | collective-permute-start | bytes 540680 | tf_op jit(solution)/shard_map/ppermute | solution.py:339
  31.7 11.1 %collective-permute-start.6 = (f32[176,256]{1,0:T(8,128)S(1)}, f32[176,256]{1,0:T(8,128)S(1)}, u32[]{:S(2)}, u32[]{:S(2)}) collective-permute-start(f32[176,256]{1,0:T(8,128)S(1)} %get-tuple-element.53), channel_id=1, source_target_pairs={{0,8},{4,12},{8,0},{12,4},{16,24},{20,28},{24,16},{28,20},{1,9},{5... | collective-permute-start | bytes 540680 | tf_op jit(solution)/shard_map/ppermute | solution.py:339
  35.8 11.2 %collective-permute-start.12 = (f32[192,128]{1,0:T(8,128)S(1)}, f32[192,128]{1,0:T(8,128)S(1)}, u32[]{:S(2)}, u32[]{:S(2)}) collective-permute-start(f32[192,128]{1,0:T(8,128)S(1)} %get-tuple-element.67), channel_id=1, source_target_pairs={{0,3},{1,2},{2,1},{3,0},{4,7},{5,6},{6,5},{7,4},{8,11},{9,10},{10,... | collective-permute-start | bytes 294920 | tf_op jit(solution)/shard_map/ppermute | solution.py:339
  39.5 7.8 %collective-permute-start.13 = (f32[192,128]{1,0:T(8,128)S(1)}, f32[192,128]{1,0:T(8,128)S(1)}, u32[]{:S(2)}, u32[]{:S(2)}) collective-permute-start(f32[192,128]{1,0:T(8,128)S(1)} %get-tuple-element.68), channel_id=1, source_target_pairs={{0,2},{1,3},{2,0},{3,1},{4,6},{5,7},{6,4},{7,5},{8,10},{9,11},{10,... | collective-permute-start | bytes 294920 | tf_op jit(solution)/shard_map/ppermute | solution.py:339
  39.6 7.7 %collective-permute-start.14 = (f32[192,128]{1,0:T(8,128)S(1)}, f32[192,128]{1,0:T(8,128)S(1)}, u32[]{:S(2)}, u32[]{:S(2)}) collective-permute-start(f32[192,128]{1,0:T(8,128)S(1)} %get-tuple-element.69), channel_id=1, source_target_pairs={{0,1},{1,0},{2,3},{3,2},{4,5},{5,4},{6,7},{7,6},{8,9},{9,8},{10,11... | collective-permute-start | bytes 294920 | tf_op jit(solution)/shard_map/ppermute | solution.py:339
  42.8 16.1 %collective-permute-start.7 = (f32[112,256]{1,0:T(8,128)S(1)}, f32[112,256]{1,0:T(8,128)S(1)}, u32[]{:S(2)}, u32[]{:S(2)}) collective-permute-start(f32[112,256]{1,0:T(8,128)S(1)} %get-tuple-element.56), channel_id=1, source_target_pairs={{0,1},{1,0},{2,3},{3,2},{4,5},{5,4},{6,7},{7,6},{8,9},{9,8},{10,11... | collective-permute-start | bytes 344072 | tf_op jit(solution)/shard_map/ppermute | solution.py:339
  44.5 14.4 %collective-permute-start.8 = (f32[112,256]{1,0:T(8,128)S(1)}, f32[112,256]{1,0:T(8,128)S(1)}, u32[]{:S(2)}, u32[]{:S(2)}) collective-permute-start(f32[112,256]{1,0:T(8,128)S(1)} %get-tuple-element.57), channel_id=1, source_target_pairs={{0,2},{1,3},{2,0},{3,1},{4,6},{5,7},{6,4},{7,5},{8,10},{9,11},{10,... | collective-permute-start | bytes 344072 | tf_op jit(solution)/shard_map/ppermute | solution.py:339
  47.1 11.9 %collective-permute-start.9 = (f32[112,256]{1,0:T(8,128)S(1)}, f32[112,256]{1,0:T(8,128)S(1)}, u32[]{:S(2)}, u32[]{:S(2)}) collective-permute-start(f32[112,256]{1,0:T(8,128)S(1)} %get-tuple-element.58), channel_id=1, source_target_pairs={{0,3},{1,2},{2,1},{3,0},{4,7},{5,6},{6,5},{7,4},{8,11},{9,10},{10,... | collective-permute-start | bytes 344072 | tf_op jit(solution)/shard_map/ppermute | solution.py:339
